TPU v7x, 128 devices: a whole 4x4x4 slice. The times are simulated.
128 devices in a mesh: dp: 2 (over z_lo), fsdp: 64 (over y, z_hi, x, core).
Axes of the slice: x: 4, y: 4, z: 4 (z_hi: 2, z_lo: 2; z = z_hi * 2 + z_lo), core: 2. Of those that a mesh axis runs over, the one named last changes fastest.
Arguments:
- attention_out: bfloat16 [65536, 2560], P(('dp', 'fsdp')), may hold values from -24 to 24
- residual: bfloat16 [65536, 2560], P(('dp', 'fsdp')), may hold values from -6 to 6
- target_rows: bfloat16 [65536, 2560], P(('dp', 'fsdp')), may hold values from -0.125 to 0.125
- ref_logit: float32 [128, 512], P(('dp', 'fsdp')), may hold values from -9 to 9
- loss_weight: int32 [128, 512], P(('dp', 'fsdp')), may hold values from -2 to 2
- segment: int32 [128, 512], P(('dp', 'fsdp')), may hold values from 0 to 15, as said below
- counts: int32 [128], P(('dp', 'fsdp')), may hold values from 64 to 512, as said below
- out_weight: bfloat16 [2560, 2560], P('fsdp'), may hold values from -0.125 to 0.125
- norm_gain: float32 [2560], replicated, may hold values from 0.25 to 1.75
Outputs:
- grad_out_weight: float32 [2560, 2560], P('fsdp')
- grad_gain: float32 [2560], replicated
- grad_attention: bfloat16 [65536, 2560], P(('dp', 'fsdp'))
- loss: float32 [], replicated
Inputs may be any that keep to these rules, and one draw needn't show every extreme that they name: `counts`: slots at or past a device's count are padding and carry no loss; at least one device is full. `segment`: is non-decreasing along each device's slots; documents do not cross devices.
All inputs are finite; a program needn't handle non-finite values.
Results may differ from a plain program's by a relative error of at most 0.0049.
Values may be sent and summed in bfloat16 or wider, within the bound.
A program may use at most 192 MiB of HBM per device.

v0:
```python
import jax
import jax.numpy as jnp
from jax import lax
from jax.sharding import PartitionSpec as P

SEGS = 16


npo_beta = 0.1
loss_scale = 1024.0


def local_pass(
    attention_rows,
    residual_rows,
    target,
    ref_row,
    weight_row,
    segment_row,
    out_weight,
    norm_gain,
    denominator,
):
    projected = jnp.dot(attention_rows, out_weight, preferred_element_type=jnp.float32)
    norm_scale = jnp.sqrt(jnp.mean(projected * projected, axis=1, keepdims=True) + 1e-06)
    normed = projected / norm_scale
    target_f = target.astype(jnp.float32)
    output_rows = residual_rows.astype(jnp.float32) + norm_gain[None, :] * normed
    target_score = jnp.sum(output_rows * target_f, axis=1)
    forget_weight = jnp.maximum(-weight_row, 0).astype(jnp.float32)
    retain_weight = jnp.maximum(weight_row, 0).astype(jnp.float32)
    segment_table = (segment_row[:, None] == jnp.arange(SEGS, dtype=jnp.int32)[None, :]).astype(
        jnp.float32
    )
    seg_sum = jnp.dot(
        forget_weight * (target_score - ref_row), segment_table, precision=lax.Precision.HIGHEST
    )
    has_forget = jnp.dot(forget_weight, segment_table, precision=lax.Precision.HIGHEST) > 0.5
    npo_total = jnp.sum(
        jnp.where(has_forget, 2.0 / npo_beta * jax.nn.softplus(npo_beta * seg_sum), 0.0)
    )
    loss_total = npo_total - jnp.sum(retain_weight * target_score)
    slot_sigmoid = jnp.dot(
        segment_table, jax.nn.sigmoid(npo_beta * seg_sum), precision=lax.Precision.HIGHEST
    )
    score_grad = loss_scale / denominator * (forget_weight * 2.0 * slot_sigmoid - retain_weight)
    output_grad = score_grad[:, None] * target_f
    gain_part = jnp.sum(output_grad * normed, axis=0)
    normed_grad = output_grad * norm_gain[None, :]
    projected_grad = (
        (normed_grad - normed * jnp.mean(normed_grad * normed, axis=1, keepdims=True)) / norm_scale
    ).astype(jnp.bfloat16)
    grad_rows = lax.dot_general(
        projected_grad, out_weight, (((1,), (1,)), ((), ())), preferred_element_type=jnp.float32
    ).astype(jnp.bfloat16)
    return (grad_rows, projected_grad, gain_part, loss_total)


def shards(
    attention_out,
    residual,
    target_rows,
    ref_logit,
    loss_weight,
    segment,
    counts,
    out_weight,
    norm_gain,
):
    capacity = attention_out.shape[0]
    live_slot = jnp.arange(capacity, dtype=jnp.int32) < counts[0]
    weight_row = jnp.where(live_slot, loss_weight[0], 0)
    magnitude = jnp.sum(jnp.abs(weight_row)).astype(jnp.float32)
    denominator = jnp.maximum(lax.psum(magnitude, ("dp", "fsdp")), 1.0)
    full_weight = lax.all_gather(out_weight, "fsdp", axis=0, tiled=True)
    grad_rows, projected_grad, gain_part, loss_total = local_pass(
        attention_out,
        residual,
        target_rows,
        ref_logit[0],
        weight_row,
        segment[0],
        full_weight,
        norm_gain,
        denominator,
    )
    grad_norm, loss_sum = lax.psum((gain_part, loss_total), ("dp", "fsdp"))
    shard_grad = lax.psum_scatter(
        lax.dot_general(
            attention_out,
            projected_grad,
            (((0,), (0,)), ((), ())),
            preferred_element_type=jnp.float32,
        ),
        "fsdp",
        scatter_dimension=0,
        tiled=True,
    )
    grad_weight = lax.psum(shard_grad, "dp")
    return (grad_weight, grad_norm, grad_rows, loss_sum / denominator)


def solution(mesh):
    placed = (
        P(("dp", "fsdp"), None),
        P(("dp", "fsdp"), None),
        P(("dp", "fsdp"), None),
        P(("dp", "fsdp"), None),
        P(("dp", "fsdp"), None),
        P(("dp", "fsdp"), None),
        P(("dp", "fsdp")),
        P("fsdp", None),
        P(),
    )
    return jax.shard_map(
        shards,
        mesh=mesh,
        in_specs=placed,
        out_specs=(P("fsdp", None), P(), P(("dp", "fsdp"), None), P()),
        check_vma=False,
    )
```

profile of v0, /device:TPU:1, one launch (start us, length us, event | category | flops | bytes accessed | tf_op | source)
XLA Modules:
  0.0 632.9 jit_solution(7528255831979755833)
XLA Ops:
  7.2 0.0 copy-start
  7.2 0.0 all-gather.2.cloned.1.call-start
  7.2 0.7 all-gather.2.cloned.1.call-update
  7.9 0.0 reduce-scatter.4.cloned.1.call-start
  8.6 1.3 maximum_convert_fusion
  10.6 71.0 %psum.28 = f32[]{:T(128)} all-reduce(f32[]{:T(128)S(6)} %convert_element_type.22), channel_id=1, replica_groups=mesh['dp'=2,'fsdp'=64] {'dp','fsdp'}, use_global_device_ids=true, to_apply=%region_1.2 | all-reduce | flops 1 | bytes 8 | tf_op jit(solution)/shard_map/psum | solution.py:74
  82.3 0.0 copy-start.5
  82.3 28.7 %all-gather.2.cloned.1.call-done = bf16[2560,2560]{1,0:T(8,128)(2,1)} async-done(((bf16[40,2560]{1,0:T(8,128)(2,1)}), bf16[2560,2560]{1,0:T(8,128)(2,1)}) %all-gather.2.cloned.1.call-update) | async-done | bytes 13107216 | tf_op jit(solution)/shard_map/all_gather | solution.py:75
  111.0 10.4 %multiply_reduce_fusion = (f32[512]{0:T(512)S(1)}, f32[512,2560]{1,0:T(8,128)S(1)}) fusion(bf16[512,2560]{1,0:T(8,128)(2,1)S(1)} %copy-done, bf16[2560,2560]{1,0:T(8,128)(2,1)} %all-gather.2.cloned.1.call-done), kind=kOutput, calls=%fused_computation.11 | convolution fusion | flops 6713507328 | bytes 20973568 | tf_op jit(solution)/shard_map/dot_general | solution.py:24
  121.5 0.0 copy-start.6
  121.5 0.0 copy-start.7
  121.5 0.0 copy-start.8
  121.5 1.4 fusion.7
  122.9 0.0 copy-done.7
  122.9 0.7 multiply_reduce_fusion.1
  123.6 0.3 fusion.9
  123.9 0.3 fusion.13
  124.3 2.0 fusion.6
  126.3 0.0 copy-done.2
  126.3 12.7 %convolution_bitcast_fusion = f32[2560,2560]{0,1:T(8,128)} fusion(bf16[512,2560]{1,0:T(8,128)(2,1)S(1)} %copy-done, bf16[512,2560]{1,0:T(8,128)(2,1)S(1)} %copy-done.3, f32[512]{0:T(512)S(1)} %broadcast_multiply_fusion, f32[512]{0:T(512)S(1)} %subtract_multiply_fusion, f32[512]{0:T(512)S(1)} %add_sqrt_fusion, f32[2560]{0:T(1024)S(1)} %copy-done.5, ...), kind=kOutput, calls=%fused_computation | convolution fusion | flops 6721372160 | bytes 36716544 | tf_op jit(solution)/shard_map/dot_general | solution.py:89
  139.1 27.4 %copy.15 = f32[2560,2560]{1,0:T(8,128)} copy(f32[2560,2560]{0,1:T(8,128)} %convolution_bitcast_fusion) | data formatting | bytes 52428800
  166.4 0.0 reduce-scatter.4.cloned.1.call-update
  166.4 0.2 all-reduce.3.cloned.1.call-start
  166.7 365.8 %reduce-scatter.4.cloned.1.call-done = f32[40,2560]{1,0:T(8,128)} async-done(((f32[2560,2560]{1,0:T(8,128)}), f32[40,2560]{1,0:T(8,128)}) %reduce-scatter.4.cloned.1.call-update) | async-done | bytes 409616
  532.4 2.5 copy.16
  534.9 0.0 all-reduce.3.cloned.1.call-update
  534.9 0.0 copy-start.1
  534.9 14.5 %convolution_convert_fusion = bf16[512,2560]{1,0:T(8,128)(2,1)} fusion(bf16[2560,2560]{1,0:T(8,128)(2,1)} %all-gather.2.cloned.1.call-done, bf16[512,2560]{1,0:T(8,128)(2,1)} %param.11, f32[512]{0:T(512)S(1)} %broadcast_multiply_fusion, f32[512]{0:T(512)S(1)} %subtract_multiply_fusion, f32[512]{0:T(512)S(1)} %add_sqrt_fusion, f32[2560]{0:T(1024)S(1)} %copy-done.5, ...), kind=kOutput, calls=%fused_computation.13 | convolution fusion | flops 6722682880 | bytes 23609344 | tf_op jit(solution)/shard_map/dot_general | solution.py:53
  549.4 0.9 fusion.12
  551.6 70.5 %all-reduce = (f32[2560]{0:T(1024)}, f32[]{:T(128)}) all-reduce(f32[2560]{0:T(1024)S(1)} %get-tuple-element.12, f32[]{:T(128)S(6)} %sub.15), channel_id=1, replica_groups=mesh['dp'=2,'fsdp'=64] {'dp','fsdp'}, use_global_device_ids=true, to_apply=%region_8.9 | all-reduce | flops 2561 | bytes 20488 | tf_op jit(solution)/shard_map/psum | solution.py:87
  622.7 0.0 all-reduce.3.cloned.1.call-done
  622.8 2.4 copy.14
  (13 shorter events, 0.1 us)
Async XLA Ops:
  7.2 103.8 %copy-start = (bf16[512,2560]{1,0:T(8,128)(2,1)S(1)}, bf16[512,2560]{1,0:T(8,128)(2,1)}, u32[]{:S(2)}) copy-start(bf16[512,2560]{1,0:T(8,128)(2,1)} %param.9) | copy-start | bytes 7864324
  7.2 103.8 %all-gather.2.cloned.1.call-start = ((), (), s32[]{:S(2)}) async-start(), calls=%async_computation.1 | async-start | bytes 13312000 | tf_op jit(solution)/shard_map/all_gather | solution.py:75
  7.9 524.5 %reduce-scatter.4.cloned.1.call-start = ((), (), s32[]{:S(2)}) async-start(), calls=%async_computation.3 | async-start | bytes 26624000
  82.3 39.1 %copy-start.5 = (f32[2560]{0:T(1024)S(1)}, f32[2560]{0:T(1024)}, u32[]{:S(2)}) copy-start(f32[2560]{0:T(1024)} %param.17) | copy-start | bytes 30724
  111.0 10.4 %copy-start.3 = (bf16[512,2560]{1,0:T(8,128)(2,1)S(1)}, bf16[512,2560]{1,0:T(8,128)(2,1)}, u32[]{:S(2)}) copy-start(bf16[512,2560]{1,0:T(8,128)(2,1)} %param.11) | copy-start | bytes 7864324
  111.0 10.4 %copy-start.4 = (bf16[512,2560]{1,0:T(8,128)(2,1)S(1)}, bf16[512,2560]{1,0:T(8,128)(2,1)}, u32[]{:S(2)}) copy-start(bf16[512,2560]{1,0:T(8,128)(2,1)} %param.10) | copy-start | bytes 7864324
  121.4 4.9 copy-start.2
  121.5 1.4 copy-start.6
  121.5 1.4 copy-start.7
  121.5 2.2 copy-start.8
  166.4 456.3 %all-reduce.3.cloned.1.call-start = ((), (), s32[]{:S(2)}) async-start(), calls=%async_computation.2 | async-start | bytes 2621440 | tf_op jit(solution)/shard_map/psum | solution.py:99
  534.9 90.3 %copy-start.1 = (bf16[512,2560]{1,0:T(8,128)(2,1)S(1)}, bf16[512,2560]{1,0:T(8,128)(2,1)}, u32[]{:S(2)}) copy-start(bf16[512,2560]{1,0:T(8,128)(2,1)} %param.9) | copy-start | bytes 7864324
Sparse Core Ops, SparseCore 0:
  11.1 99.8 all-gather.1
  166.6 365.8 reduce-scatter.3
  535.1 55.1 all-reduce.2
where the time goes:
time: 634 us; the launch traced here: 633 us
  waiting for transfers between devices  395 us (62%)
  blocking collectives  141 us (22%)
  matrix products  39.1 us (6%)
  local copies, waits for them, and re-layouts  32.3 us (5%)
  between operations  19 us (3%)
    unnamed x4, waiting for transfers between devices  366 us
    psum x1, blocking collectives, shards(): denominator = jnp.maximum(lax.psum(magnitude, ('dp', 'fsdp')), 1.0)  71 us
    psum x1, blocking collectives, shards(): grad_norm, loss_sum = lax.psum((gain_part, loss_total), ('dp', 'fsdp'))  70.5 us
    unnamed x21, local copies, waits for them, and re-layouts  32.3 us
    all_gather x1, waiting for transfers between devices, shards(): full_weight = lax.all_gather(out_weight, 'fsdp', axis=0, tiled=True)  28.7 us
    dot_general x1, matrix products, local_pass(): lax.dot_general(projected_grad, out_weight, (((1,), (1,)), ((), ())), pre...  14.5 us
    dot_general x1, matrix products, shards(): lax.dot_general(attention_out, projected_grad, (((0,), (0,)), ((), ())),...  12.7 us
  transfers between devices with their start and end apart: 3, of which 2 were waited for; matrix products, arithmetic and copies ran while one was open for 3% of the time, Pallas kernels for 0%

commit v1 on v0

v1 whole, which is shorter than its diff:
```python
import functools

import jax
import jax.numpy as jnp
from jax import lax
from jax.experimental import pallas as pl
from jax.experimental.pallas import tpu as pltpu
from jax.sharding import PartitionSpec as P

SEGS = 16
F32 = jnp.float32
BF16 = jnp.bfloat16
MESH = pl.DeviceIdType.MESH

npo_beta = 0.1
loss_scale = 1024.0

ROW = 80
HALF = 40
CAP = 512
DW = 2560
HC = 1280
GW = 256
NG = HC // GW
WIDTH = (256, 256, 128)
ORDER = (0, 1, 3, 2)


def place():
    dp = lax.axis_index("dp")
    f = lax.axis_index("fsdp")
    return (f // 2) % 4, f // 16, ((f // 8) % 2) * 2 + dp, f % 2


def device(x, y, z, c):
    return (z % 2, ((y * 2 + z // 2) * 4 + x) * 2 + c)


def kernel(
    a_hbm,
    r_hbm,
    t_hbm,
    ref_ref,
    lw_ref,
    seg_ref,
    cnt_ref,
    w_ref,
    gain_ref,
    gw_out,
    gg_out,
    ga_out,
    loss_out,
    a2,
    at,
    t2,
    r2,
    wg,
    pr,
    pg,
    wx,
    meta,
    acc1,
    acc2,
    acc3,
    sp,
    alpha,
    beta,
    den,
    gsum,
    gsib,
    st_o0, st_o1, st_o2,
    st_n0, st_n1, st_n2,
    rl0, rl1, rl2,
    rv0, rv1, rv2,
    ow0, ow1, ow2,
    s20, s21, s22,
    v20, v21, v22,
    s30, s31, s32,
    v30, v31, v32,
    fb,
    fr,
    ga_send,
    ga_recv,
    ga_own,
    loc,
    sib_s, sib_r,
    den_s, den_r,
    g_s, g_r,
    p1_s, p1_r,
    p2_s, p2_r,
    p3_s, p3_r,
    p4_s, p4_r,
    q0_s, q0_r,
    q1_s, q1_r,
    q2_s, q2_r,
    q3_s, q3_r,
    qf_s, qf_r,
):
    st_o = (st_o0, st_o1, st_o2)
    st_n = (st_n0, st_n1, st_n2)
    rl = (rl0, rl1, rl2)
    rv = (rv0, rv1, rv2)
    own = (ow0, ow1, ow2)
    s2 = (s20, s21, s22)
    v2 = (v20, v21, v22)
    s3 = (s30, s31, s32)
    v3 = (v30, v31, v32)
    x, y, z, c = place()
    zl = z % 2
    sib = device(x, y, z, 1 - c)
    pieces = range(3)
    yz = (None, (1 - c, c), (c, 1 - c))

    def pos(p):
        if p == 0:
            return y, z, x
        m, n = yz[p]
        return x, z * m + y * n, y * m + z * n

    def coords(p, p1, p2, p3):
        if p == 0:
            return p3, p1, p2
        m, n = yz[p]
        return p1, p3 * m + p2 * n, p2 * m + p3 * n

    def peer(p, d1, d2, d3):
        p1, p2, p3 = pos(p)
        return device(*coords(p, (p1 + d1) % 4, (p2 + d2) % 4, (p3 + d3) % 4), c)

    def wslot(p, a3, a2_, start, n):
        bx, by, bz = coords(p, 0, a2_, a3)
        if p == 0:
            return wg.at[bz % 2, pl.ds(start, n), bz // 2, bx]
        if p == 1:
            return wg.at[2 + bz % 2, by, bz // 2, pl.ds(start, n)]
        return wg.at[4, by, bz // 2, pl.ds(start, n), :, pl.ds(pl.multiple_of((bz % 2) * 128, 128), 128)]

    def remote(src, dst, ss, rs, dev):
        return pltpu.make_async_remote_copy(
            src_ref=src, dst_ref=dst, send_sem=ss, recv_sem=rs, device_id=dev, device_id_type=MESH
        )

    mine = pl.ds(pl.multiple_of(c * HC, 128), HC)
    theirs = pl.ds(pl.multiple_of((1 - c) * HC, 128), HC)
    loads = [
        pltpu.make_async_copy(a_hbm, a2.at[0], loc.at[0]),
        pltpu.make_async_copy(t_hbm.at[:, mine], t2.at[0], loc.at[1]),
        pltpu.make_async_copy(r_hbm.at[:, mine], r2.at[0], loc.at[2]),
    ]
    for copy in loads:
        copy.start()

    partners = [sib, device(x, y, z + 1 - 2 * zl, 1 - c)]
    for d in (1, 2, 3):
        partners.append(device((x + d) % 4, y, z, c))
        partners.append(device(x, (y + d) % 4, z, c))
        partners.append(device(x, y, (z + d) % 4, c))
    barrier = pltpu.get_barrier_semaphore()
    for q in partners:
        pl.semaphore_signal(barrier, inc=1, device_id=q, device_id_type=MESH)

    lane = lax.broadcasted_iota(jnp.int32, (1, CAP), 1)
    live = lane < cnt_ref[0]
    weight = jnp.where(live, lw_ref[...], 0).astype(F32)
    magnitude = jnp.sum(jnp.abs(weight), axis=1, keepdims=True)
    rows8 = lax.broadcasted_iota(jnp.int32, (8, CAP), 0)
    meta[0] = jnp.where(
        rows8 == 0,
        jnp.broadcast_to(ref_ref[...], (8, CAP)),
        jnp.where(
            rows8 == 1,
            jnp.broadcast_to(weight, (8, CAP)),
            jnp.where(
                rows8 == 2,
                jnp.broadcast_to(seg_ref[...].astype(F32), (8, CAP)),
                jnp.broadcast_to(magnitude, (8, CAP)),
            ),
        ),
    )

    def shard_columns(core):
        base = core * HC
        return jnp.concatenate(
            [
                w_ref[:, pl.ds(pl.multiple_of(base + zl * 256, 128), 256)].astype(F32),
                w_ref[:, pl.ds(pl.multiple_of(base + 512 + zl * 256, 128), 256)].astype(F32),
                w_ref[:, pl.ds(pl.multiple_of(base + 1024 + zl * 128, 128), 128)].astype(F32),
            ],
            axis=1,
        )

    wx[0] = shard_columns(1 - c)
    pl.semaphore_wait(barrier, len(partners))

    sib_w = remote(wx.at[0], wx.at[1], sib_s.at[0], sib_r.at[0], sib)
    sib_m = remote(meta.at[0], meta.at[1], sib_s.at[1], sib_r.at[1], sib)
    sib_a = remote(a_hbm, a2.at[1], sib_s.at[2], sib_r.at[2], sib)
    sib_t = remote(t_hbm.at[:, theirs], t2.at[1], sib_s.at[3], sib_r.at[3], sib)
    sib_res = remote(r_hbm.at[:, theirs], r2.at[1], sib_s.at[4], sib_r.at[4], sib)
    for copy in (sib_w, sib_m, sib_a, sib_t, sib_res):
        copy.start()

    own_w = shard_columns(c)
    sib_w.wait_recv()
    got_w = wx[1]
    first = c == 0
    block = jnp.concatenate(
        [jnp.where(first, own_w, got_w), jnp.where(first, got_w, own_w)], axis=0
    ).astype(BF16)
    bx0, by0, bz0 = x, y, z // 2
    wg[zl, by0, bz0, bx0] = block[:, 0:256]
    wg[2 + zl, by0, bz0, bx0] = block[:, 256:512]
    wg[4, by0, bz0, bx0, :, pl.ds(pl.multiple_of(zl * 128, 128), 128)] = block[:, 512:640]

    ph1, ph2, ph3, ph4 = {}, {}, {}, {}
    for p in pieces:
        p1, p2, p3 = pos(p)
        for d in (1, 2, 3):
            slot = wslot(p, p3, p2, p1, 1)
            ph1[p, d] = remote(slot, slot, p1_s.at[p, d - 1], p1_r.at[p, d - 1], peer(p, d, 0, 0))
            line = wslot(p, p3, p2, 0, 4)
            ph2[p, d] = remote(line, line, p2_s.at[p, d - 1], p2_r.at[p, d - 1], peer(p, 0, d, 0))
        for d in range(4):
            a2_ = (p2 + d) % 4
            line = wslot(p, p3, a2_, 0, 4)
            low = wslot(p, (p3 + 3) % 4, a2_, 0, 2)
            high = wslot(p, (p3 + 1) % 4, a2_, 2, 2)
            ph3[p, d, 0] = remote(line, line, p3_s.at[p, d, 0], p3_r.at[p, d, 0], peer(p, 0, 0, 1))
            ph3[p, d, 1] = remote(line, line, p3_s.at[p, d, 1], p3_r.at[p, d, 1], peer(p, 0, 0, 3))
            ph4[p, d, 0] = remote(low, low, p4_s.at[p, d, 0], p4_r.at[p, d, 0], peer(p, 0, 0, 1))
            ph4[p, d, 1] = remote(high, high, p4_s.at[p, d, 1], p4_r.at[p, d, 1], peer(p, 0, 0, 3))

    sends = [sib_w, sib_m, sib_a, sib_t, sib_res]

    def start(copy):
        copy.start()
        sends.append(copy)

    for d in (1, 3, 2):
        for p in pieces:
            start(ph1[p, d])

    def den_phase(axis, value):
        at_ = (x, y, z)[axis]
        den[axis, at_] = value
        copies = []
        for d in (1, 2, 3):
            q = [x, y, z]
            q[axis] = (at_ + d) % 4
            slot = den.at[axis, at_]
            copy = remote(
                slot, slot, den_s.at[axis, d - 1], den_r.at[axis, d - 1], device(q[0], q[1], q[2], c)
            )
            start(copy)
            copies.append(copy)
        return copies

    def den_total(axis, copies):
        for copy in copies:
            copy.wait_recv()
        return den[axis, 0] + den[axis, 1] + den[axis, 2] + den[axis, 3]

    sib_m.wait_recv()
    den_copies = den_phase(0, meta[0, :, 0:128] * 0 + (meta[0, 3:4, 0:128] + meta[1, 3:4, 0:128]))

    def transpose_rows(slot):
        @pl.loop(0, DW // 128)
        def _(k):
            off = pl.ds(pl.multiple_of(k * 128, 128), 128)
            at[off, slot * CAP : (slot + 1) * CAP] = a2[slot, :, off].T

    for copy in loads:
        copy.wait()

    for p in pieces:
        for d in (1, 3, 2):
            ph1[p, d].wait_recv()
        for d in (1, 3, 2):
            start(ph2[p, d])
        start(ph3[p, 0, 0])
        start(ph3[p, 0, 1])

    den_copies = den_phase(1, den_total(0, den_copies))
    transpose_rows(0)

    for j in (1, 2, 3):
        d, before = ORDER[j], ORDER[j - 1]
        for p in pieces:
            ph2[p, 4 - d].wait_recv()
            start(ph3[p, d, 0])
            start(ph3[p, d, 1])
        for p in pieces:
            for s in (0, 1):
                ph3[p, before, s].wait_recv()
                start(ph4[p, before, s])
        if j == 1:
            den_copies = den_phase(2, den_total(1, den_copies))
            sib_a.wait_recv()
            transpose_rows(1)
        if j == 2:
            sib_t.wait_recv()
            sib_res.wait_recv()
            for slot in (0, 1):
                part = jnp.zeros((CAP, 128), F32)
                for k in range(HC // 128):
                    cols = slice(k * 128, (k + 1) * 128)
                    part += t2[slot, :, cols].astype(F32) * r2[slot, :, cols].astype(F32)
                acc2[slot] = part
            for slot in (0, 1):
                acc1[slot] = jnp.zeros((CAP, 128), F32)
                acc3[slot] = jnp.zeros((CAP, 128), F32)
    for p in pieces:
        for s in (0, 1):
            ph3[p, ORDER[3], s].wait_recv()
            start(ph4[p, ORDER[3], s])
    denominator = jnp.maximum(den_total(2, den_copies)[0:1, 0:1], 1.0)
    for p in pieces:
        for d in ORDER:
            for s in (0, 1):
                ph4[p, d, s].wait_recv()

    @pl.loop(0, NG)
    def _(g):
        cols = pl.ds(pl.multiple_of(g * GW, GW), GW)
        gains = gain_ref[:, pl.ds(pl.multiple_of(c * HC + g * GW, GW), GW)]
        w = wg[g].reshape(DW, GW)

        @pl.loop(0, 2)
        def _(slot):
            res = jnp.dot(a2[slot], w, preferred_element_type=F32)
            pr[g, slot] = res
            sq = res * res
            acc1[slot] += sq[:, :128] + sq[:, 128:]
            tp = res * t2[slot, :, cols].astype(F32) * gains
            acc3[slot] += tp[:, :128] + tp[:, 128:]

    lanes = lax.broadcasted_iota(jnp.int32, (CAP, 128), 1)

    @pl.loop(0, 2)
    def _(slot):
        q1 = jnp.sum(acc1[slot], axis=1, keepdims=True)
        q2 = jnp.sum(acc2[slot], axis=1, keepdims=True)
        q3 = jnp.sum(acc3[slot], axis=1, keepdims=True)
        sp[0, slot] = jnp.where(lanes == 0, q1, jnp.where(lanes == 1, q2, q3))

    stat = [
        remote(sp.at[0, s], sp.at[1, 1 - s], sib_s.at[5 + s], sib_r.at[5 + s], sib) for s in (0, 1)
    ]
    for copy in stat:
        start(copy)
    for copy in stat:
        copy.wait_recv()

    @pl.loop(0, 2)
    def _(slot):
        total = sp[0, slot] + sp[1, slot]
        q1, q2, q3 = total[:, 0:1], total[:, 1:2], total[:, 2:3]
        scale = jnp.sqrt(q1 * (1.0 / DW) + 1e-06)
        score = q2 + q3 / scale
        facts = meta[slot].T
        ref, wgt, seg = facts[:, 0:1], facts[:, 1:2], facts[:, 2:3]
        forget = jnp.maximum(-wgt, 0.0)
        retain = jnp.maximum(wgt, 0.0)
        table = (seg == lanes.astype(F32)).astype(F32)
        seg_sum = jnp.sum(table * (forget * (score - ref)), axis=0, keepdims=True)
        has = jnp.sum(table * forget, axis=0, keepdims=True) > 0.5
        scaled = npo_beta * seg_sum
        soft = jnp.maximum(scaled, 0.0) + jnp.log1p(jnp.exp(-jnp.abs(scaled)))
        npo = jnp.sum(jnp.where(has, 2.0 / npo_beta * soft, 0.0), axis=1, keepdims=True)
        loss = npo - jnp.sum(retain * score, axis=0, keepdims=True)

        @pl.when(slot == 0)
        def _():
            gsum[0, x] = jnp.zeros((8, HC + 128), F32)
            gsum[0, x, 0:1, HC : HC + 128] = jnp.broadcast_to(loss, (1, 128))

        sig = jnp.sum(table * jax.nn.sigmoid(scaled), axis=1, keepdims=True)
        grad = loss_scale / denominator * (forget * 2.0 * sig - retain)
        alpha[slot] = jnp.broadcast_to(grad / scale, (CAP, 128))
        beta[slot] = jnp.broadcast_to(q3 / (scale * scale * DW), (CAP, 128))

    @pl.loop(0, NG)
    def _(g):
        cols = pl.ds(pl.multiple_of(g * GW, GW), GW)
        gains = gain_ref[:, pl.ds(pl.multiple_of(c * HC + g * GW, GW), GW)]

        @pl.loop(0, 2)
        def _(slot):
            al = jnp.concatenate([alpha[slot], alpha[slot]], axis=1)
            be = jnp.concatenate([beta[slot], beta[slot]], axis=1)
            p_ = pr[g, slot]
            t = t2[slot, :, cols].astype(F32)
            rows = pl.ds(pl.multiple_of(slot * CAP, CAP), CAP)
            pg[g, rows] = (al * (t * gains - p_ * be)).astype(BF16)
            gsum[0, x, 0:1, cols] += jnp.sum(al * t * p_, axis=0, keepdims=True)

    def grad_blocks(p, v, emit):
        w_ = WIDTH[p]
        if p == 0:
            left = jnp.concatenate(
                [
                    at[pl.ds(pl.multiple_of((k * 4 + v) * ROW, 16), ROW), :] for k in range(8)
                ],
                axis=0,
            )
            for h in (0, 1):
                res = jnp.dot(left, pg[h], preferred_element_type=F32)
                for yy in range(4):
                    for zz in range(2):
                        k = yy * 2 + zz
                        emit(2 * zz + h, yy, res[k * ROW : (k + 1) * ROW])
            return
        m, n = yz[p]
        for h in (0, 1):
            parts = []
            for k in (0, 1):
                by = v * m + (2 * k + h) * n
                bz = k * m + (v // 2) * n
                parts.append(at[pl.ds(pl.multiple_of((by * 2 + bz) * 4 * ROW, 16), 4 * ROW), :])
            left = jnp.concatenate(parts, axis=0)
            side = h * m + (v % 2) * n
            if p == 1:
                right = pg[2 + side]
            else:
                right = pg[4, :, pl.ds(pl.multiple_of(side * 128, 128), 128)]
            res = jnp.dot(left, right, preferred_element_type=F32)
            for k in (0, 1):
                for xx in range(4):
                    i = k * 4 + xx
                    emit(2 * k + h, xx, res[i * ROW : (i + 1) * ROW])

    q0, q1, q2, q3 = {}, {}, {}, {}
    for p in pieces:
        p1, p2, p3 = pos(p)
        for s in (0, 1):
            half = pl.ds(2 * s, 2)
            to = peer(p, 0, 0, 1 + 2 * s)
            q0[p, s] = remote(st_o[p].at[:, half], rl[p].at[s], q0_s.at[p, s], q0_r.at[p, s], to)
            for d in range(4):
                i = (p2 + d) % 4
                q1[p, s, d] = remote(
                    st_n[p].at[s, i], rv[p].at[s, i], q1_s.at[p, s, d], q1_r.at[p, s, d], to
                )
        for d in (1, 2, 3):
            q2[p, d] = remote(
                s2[p].at[d - 1], v2[p].at[d - 1], q2_s.at[p, d - 1], q2_r.at[p, d - 1], peer(p, 0, d, 0)
            )
            q3[p, d] = remote(
                s3[p].at[d - 1], v3[p].at[d - 1], q3_s.at[p, d - 1], q3_r.at[p, d - 1], peer(p, d, 0, 0)
            )

    def put(ref, prefix=()):
        def emit(i, j, value):
            ref[prefix + (i, j)] = value.astype(ref.dtype)

        return emit

    for p in pieces:
        grad_blocks(p, (pos(p)[2] + 2) % 4, put(st_o[p]))
        start(q0[p, 0])
        start(q0[p, 1])

    def gain_phase(axis):
        at_ = (x, y, z)[axis]
        copies = []
        for d in (1, 2, 3):
            q = [x, y, z]
            q[axis] = (at_ + d) % 4
            slot = gsum.at[axis, at_]
            copy = remote(
                slot, slot, g_s.at[axis, d - 1], g_r.at[axis, d - 1], device(q[0], q[1], q[2], c)
            )
            start(copy)
            copies.append(copy)
        return copies

    def gain_total(axis, copies):
        for copy in copies:
            copy.wait_recv()
        return (gsum[axis, 0] + gsum[axis, 1]) + (gsum[axis, 2] + gsum[axis, 3])

    gain_copies = gain_phase(0)

    for p in pieces:
        grad_blocks(p, pos(p)[2], put(own[p]))

    gsum[1, y] = gain_total(0, gain_copies)
    gain_copies = gain_phase(1)

    for p in pieces:
        p2 = pos(p)[1]
        for s in (0, 1):
            q0[p, s].wait_recv()

            def emit(i, j, value, p=p, s=s):
                if j // 2 == s:
                    value = value + rl[p][s, i, j % 2].astype(F32)
                st_n[p][s, i, j] = value.astype(BF16)

            grad_blocks(p, (pos(p)[2] + 1 + 2 * s) % 4, emit)
            for d in (2, 1, 3, 0):
                start(q1[p, s, d])

    gsum[2, z] = gain_total(1, gain_copies)
    gain_copies = gain_phase(2)

    def grad_rows(slot, yy):
        res = jnp.zeros((CAP, 640), F32)
        for g in range(NG):
            w = wg[g, yy].reshape(640, GW)
            res = res + lax.dot_general(
                pg[g, slot * CAP : (slot + 1) * CAP],
                w,
                (((1,), (1,)), ((), ())),
                preferred_element_type=F32,
            )
        return res

    @pl.loop(0, 4)
    def _(yy):
        ga_send[:, pl.ds(pl.multiple_of(yy * 640, 128), 640)] = grad_rows(1, yy).astype(BF16)

    ga_copy = remote(ga_send, ga_recv, sib_s.at[7], sib_r.at[7], sib)
    start(ga_copy)

    def reduce_step(d):
        for p in pieces:
            p1, p2, p3 = pos(p)
            i = (p2 + d) % 4
            for s in (0, 1):
                q1[p, s, d].wait_recv()
            total = own[p][i] + rv[p][0, i].astype(F32) + rv[p][1, i].astype(F32)
            if d == 0:
                own[p][i] = total
            else:
                s2[p][d - 1] = total.astype(BF16)
                start(q2[p, d])

    reduce_step(2)
    reduce_step(1)

    ga_copy.wait_recv()

    @pl.loop(0, 4)
    def _(yy):
        cols = pl.ds(pl.multiple_of(yy * 640, 128), 640)
        ga_own[:, cols] = (grad_rows(0, yy) + ga_recv[:, cols].astype(F32)).astype(BF16)

    ga_store = pltpu.make_async_copy(ga_own, ga_out, loc.at[3])
    ga_store.start()

    reduce_step(3)
    reduce_step(0)

    total = gain_total(2, gain_copies)
    gsib[c] = total
    gcopy = remote(gsib.at[c], gsib.at[c], sib_s.at[8], sib_r.at[8], sib)
    start(gcopy)

    for p in pieces:
        p1, p2, p3 = pos(p)
        acc = own[p][p2]
        for d in (1, 3, 2):
            q2[p, d].wait_recv()
            acc = acc + v2[p][d - 1].astype(F32)
        own[p][p2] = acc
        for d in (1, 3, 2):
            s3[p][d - 1] = own[p][p2, (p1 + d) % 4].astype(BF16)
            start(q3[p, d])

    offs = (0, 256, 512)
    for p in pieces:
        p1, p2, p3 = pos(p)
        acc = own[p][p2, p1]
        for d in (1, 3, 2):
            q3[p, d].wait_recv()
            acc = acc + v3[p][d - 1].astype(F32)
        fb[:, offs[p] : offs[p] + WIDTH[p]] = acc

    keep = pl.ds(pl.multiple_of(c * HALF, 8), HALF)
    give = pl.ds(pl.multiple_of((1 - c) * HALF, 8), HALF)
    zn = z + 1 - 2 * zl
    last = [
        remote(fb.at[give], fr.at[0], qf_s.at[0], qf_r.at[0], sib),
        remote(fb.at[keep], fr.at[1], qf_s.at[1], qf_r.at[1], device(x, y, zn, c)),
        remote(fb.at[give], fr.at[2], qf_s.at[2], qf_r.at[2], device(x, y, zn, 1 - c)),
    ]
    for copy in (last[1], last[2], last[0]):
        start(copy)

    def place_columns(core, side, value):
        base = core * HC
        gw_out[:, pl.ds(pl.multiple_of(base + side * 256, 128), 256)] = value[:, 0:256]
        gw_out[:, pl.ds(pl.multiple_of(base + 512 + side * 256, 128), 256)] = value[:, 256:512]
        gw_out[:, pl.ds(pl.multiple_of(base + 1024 + side * 128, 128), 128)] = value[:, 512:640]

    place_columns(c, zl, fb[keep])

    gcopy.wait_recv()
    for core in (0, 1):
        gg_out[:, core * HC : (core + 1) * HC] = gsib[core, 0:1, 0:HC]
    loss_out[...] = (gsib[0, 0:1, HC : HC + 128] + gsib[1, 0:1, HC : HC + 128]) / denominator

    last[0].wait_recv()
    place_columns(1 - c, zl, fr[0])
    last[1].wait_recv()
    place_columns(c, 1 - zl, fr[1])
    last[2].wait_recv()
    place_columns(1 - c, 1 - zl, fr[2])

    for copy in sends:
        copy.wait_send()
    ga_store.wait()


def scratch():
    dma = pltpu.SemaphoreType.DMA
    vm = pltpu.VMEM
    out = [
        vm((2, CAP, DW), BF16),
        vm((DW, 2 * CAP), BF16),
        vm((2, CAP, HC), BF16),
        vm((2, CAP, HC), BF16),
        vm((NG, 4, 2, 4, ROW, GW), BF16),
        vm((NG, 2, CAP, GW), F32),
        vm((NG, 2 * CAP, GW), BF16),
        vm((2, HALF, 640), F32),
        vm((2, 8, CAP), F32),
        vm((2, CAP, 128), F32),
        vm((2, CAP, 128), F32),
        vm((2, CAP, 128), F32),
        vm((2, 2, CAP, 128), F32),
        vm((2, CAP, 128), F32),
        vm((2, CAP, 128), F32),
        vm((3, 4, 8, 128), F32),
        vm((3, 4, 8, HC + 128), F32),
        vm((2, 8, HC + 128), F32),
    ]
    out += [vm((4, 4, ROW, w), BF16) for w in WIDTH]
    out += [vm((2, 4, 4, ROW, w), BF16) for w in WIDTH]
    out += [vm((2, 4, 2, ROW, w), BF16) for w in WIDTH]
    out += [vm((2, 4, 4, ROW, w), BF16) for w in WIDTH]
    out += [vm((4, 4, ROW, w), F32) for w in WIDTH]
    out += [vm((3, 4, ROW, w), BF16) for w in WIDTH]
    out += [vm((3, 4, ROW, w), BF16) for w in WIDTH]
    out += [vm((3, ROW, w), BF16) for w in WIDTH]
    out += [vm((3, ROW, w), BF16) for w in WIDTH]
    out += [
        vm((ROW, 640), F32),
        vm((3, HALF, 640), F32),
        vm((CAP, DW), BF16),
        vm((CAP, DW), BF16),
        vm((CAP, DW), BF16),
        dma((4,)),
    ]
    for shape in ((9,), (3, 3), (3, 3), (3, 3), (3, 3), (3, 4, 2), (3, 4, 2), (3, 2), (3, 2, 4), (3, 3), (3, 3), (3,)):
        out += [dma(shape), dma(shape)]
    return out


def shards(attention_out, residual, target_rows, ref_logit, loss_weight, segment, counts, out_weight, norm_gain):
    any_ = pl.BlockSpec(memory_space=pl.ANY)
    vmem = pl.BlockSpec(memory_space=pltpu.VMEM)
    smem = pl.BlockSpec(memory_space=pltpu.SMEM)
    gw, gg, ga, loss = pl.pallas_call(
        kernel,
        out_shape=(
            jax.ShapeDtypeStruct((HALF, DW), F32),
            jax.ShapeDtypeStruct((1, DW), F32),
            jax.ShapeDtypeStruct((CAP, DW), BF16),
            jax.ShapeDtypeStruct((1, 128), F32),
        ),
        in_specs=[any_, any_, any_, vmem, vmem, vmem, smem, vmem, vmem],
        out_specs=(vmem, vmem, any_, vmem),
        scratch_shapes=scratch(),
        compiler_params=pltpu.CompilerParams(
            collective_id=0, has_side_effects=True, vmem_limit_bytes=62 * 2**20
        ),
        cost_estimate=pl.CostEstimate(
            flops=3 * 2 * CAP * DW * DW, bytes_accessed=4 * CAP * DW * 2, transcendentals=0
        ),
    )(
        attention_out,
        residual,
        target_rows,
        ref_logit,
        loss_weight,
        segment,
        counts,
        out_weight,
        norm_gain.reshape(1, DW),
    )
    return gw, gg.reshape(DW), ga, loss[0, 0]


def solution(mesh):
    rows = P(("dp", "fsdp"), None)
    placed = (rows,) * 6 + (P(("dp", "fsdp")), P("fsdp", None), P())
    return jax.shard_map(
        shards,
        mesh=mesh,
        in_specs=placed,
        out_specs=(P("fsdp", None), P(), rows, P()),
        check_vma=False,
    )
```

time: 634 us -> 130 us (0.21)
  waiting for transfers between devices: 395 us -> 0 us
  blocking collectives: 141 us -> 0 us
  Pallas kernels: 0 us -> 119 us
  matrix products: 39.1 us -> 0 us
  local copies, waits for them, and re-layouts: 32.3 us -> 6.5 us
  between operations: 19 us -> 2.46 us
    unnamed x4 -> x0, waiting for transfers between devices: 366 us -> none
    psum x2 -> x0, blocking collectives: 141 us -> none  [the longest x1 71 us: shards(): denominator = jnp.maximum(lax.psum(magnitude, ('dp', 'fsdp')), 1.0)]
    pallas_call x0 -> x1, Pallas kernels: none -> 119 us  [shards(): pl.pallas_call(kernel, out_shape=(jax.ShapeDtypeStruct((HALF, DW), F32),...]
    dot_general x6 -> x0, matrix products: 39.1 us -> none  [the longest x1 14.5 us: local_pass(): lax.dot_general(projected_grad, out_weight, (((1,), (1,)), ((), ())), pre...]
    all_gather x1 -> x0, waiting for transfers between devices: 28.7 us -> none  [shards(): full_weight = lax.all_gather(out_weight, 'fsdp', axis=0, tiled=True)]
    unnamed x21 -> x4, local copies, waits for them, and re-layouts: 32.3 us -> 5.18 us
  transfers between devices with their start and end apart: 3 -> 0, of which waited for: 2 -> 0; matrix products, arithmetic and copies ran while one was open for 3% -> 0% of each run, Pallas kernels for 0% -> 0%
where the time goes in v1:
time: 130 us; the launch traced here: 129 us
  Pallas kernels  119 us (92%)
  local copies, waits for them, and re-layouts  6.5 us (5%)
  between operations  2.46 us (2%)
  other arithmetic  1.33 us (1%)
    pallas_call x1, Pallas kernels, shards(): pl.pallas_call(kernel, out_shape=(jax.ShapeDtypeStruct((HALF, DW), F32),...  119 us
    unnamed x4, local copies, waits for them, and re-layouts  5.18 us

profile of v1, /device:TPU:1, one launch (start us, length us, event | category | flops | bytes accessed | tf_op | source)
XLA Modules:
  0.0 129.5 jit_solution(17320666319452550138)
XLA Ops:
  0.6 1.3 %reshape.14.gain_ref = f32[1,2560]{1,0:T(1,128)} reshape(f32[2560]{0:T(1024)} %param.17) | data formatting | bytes 20480 | tf_op jit(solution)/shard_map/reshape | solution.py:691
  2.6 119.2 %shard_map.120 = (f32[40,2560]{1,0:T(8,128)}, f32[1,2560]{1,0:T(1,128)}, bf16[512,2560]{1,0:T(8,128)(2,1)}, f32[1,128]{1,0:T(1,128)}) custom-call(bf16[512,2560]{1,0:T(8,128)(2,1)} %a_hbm.1, bf16[512,2560]{1,0:T(8,128)(2,1)} %r_hbm.1, bf16[512,2560]{1,0:T(8,128)(2,1)} %t_hbm.1, f32[1,512]{1,0:T(1,128)} %ref_ref.1, s32[1,512]{1,0:T(1,128)} %lw_ref.1, ...), custom_call_target="tpu_custom_call" | custom-call | flops 20132659200 | bytes 10485760 | tf_op jit(solution)/shard_map/pallas_call | solution.py:665
  121.8 1.3 %reduce = f32[2560]{0:T(1024)} reduce(f32[1,2560]{1,0:T(1,128)} %get-tuple-element.9, f32[]{:T(128)} %constant.5), dimensions={0}, to_apply=%get-tuple-element.9.reduce_sub_computation | reduce | bytes 20484 | tf_op jit(solution)/shard_map/pallas_call | solution.py:665
  123.1 1.8 %copy.17 = f32[40,2560]{1,0:T(8,128)} copy(f32[40,2560]{1,0:T(8,128)} %get-tuple-element.16) | data formatting | bytes 819200
  124.9 0.0 copy-start
  124.9 3.4 %copy.18 = bf16[512,2560]{1,0:T(8,128)(2,1)} copy(bf16[512,2560]{1,0:T(8,128)(2,1)} %get-tuple-element.18) | data formatting | bytes 5242880
  128.3 0.0 copy-done
Async XLA Ops:
  124.9 3.4 %copy-start = (f32[1,128]{1,0:T(1,128)S(1)}, f32[1,128]{1,0:T(1,128)}, u32[]{:S(2)}) copy-start(f32[1,128]{1,0:T(1,128)} %get-tuple-element.11) | copy-start | bytes 1540

commit v2 on v1

v2 whole, which is shorter than its diff:
```python
import functools

import jax
import jax.numpy as jnp
from jax import lax
from jax.experimental import pallas as pl
from jax.experimental.pallas import tpu as pltpu
from jax.sharding import PartitionSpec as P

SEGS = 16
F32 = jnp.float32
BF16 = jnp.bfloat16
MESH = pl.DeviceIdType.MESH

npo_beta = 0.1
loss_scale = 1024.0

ROW = 80
HALF = 40
CAP = 512
DW = 2560
HC = 1280
GW = 256
NG = HC // GW
WIDTH = (256, 256, 128)
ORDER = (0, 1, 3, 2)
PARTS = 8


def place():
    dp = lax.axis_index("dp")
    f = lax.axis_index("fsdp")
    return (f // 2) % 4, f // 16, ((f // 8) % 2) * 2 + dp, f % 2


def device(x, y, z, c):
    return (z % 2, ((y * 2 + z // 2) * 4 + x) * 2 + c)


def kernel(
    a_hbm,
    r_hbm,
    t_hbm,
    ref_ref,
    lw_ref,
    seg_ref,
    cnt_ref,
    w_ref,
    gain_in,
    gw_out,
    gg_out,
    ga_out,
    loss_out,
    gain_row,
    gcol,
    a2,
    at,
    t2,
    r2,
    tt,
    wgp,
    wgn,
    pr,
    pg,
    wx,
    meta,
    stat,
    sp,
    alpha,
    beta,
    gacc,
    den,
    gsum,
    gsib,
    st_o0, st_o1, st_o2,
    st_n0, st_n1, st_n2,
    rl0, rl1, rl2,
    rv0, rv1, rv2,
    ow0, ow1, ow2,
    s20, s21, s22,
    v20, v21, v22,
    s30, s31, s32,
    v30, v31, v32,
    fb,
    fr,
    ga_send,
    ga_recv,
    ga_own,
    loc,
    sib_s, sib_r,
    den_s, den_r,
    g_s, g_r,
    p1_s, p1_r,
    p2_s, p2_r,
    p3_s, p3_r,
    p4_s, p4_r,
    q0_s, q0_r,
    qa_s, qa_r,
    q1_s, q1_r,
    q2_s, q2_r,
    q3_s, q3_r,
    qf_s, qf_r,
):
    st_o = (st_o0, st_o1, st_o2)
    st_n = (st_n0, st_n1, st_n2)
    rl = (rl0, rl1, rl2)
    rv = (rv0, rv1, rv2)
    own = (ow0, ow1, ow2)
    s2 = (s20, s21, s22)
    v2 = (v20, v21, v22)
    s3 = (s30, s31, s32)
    v3 = (v30, v31, v32)
    x, y, z, c = place()
    zl = z % 2
    sib = device(x, y, z, 1 - c)
    pieces = range(3)
    yz = ((1 - c, c), (1 - c, c), (c, 1 - c))

    def pos(p):
        m, n = yz[p]
        if p == 0:
            return y * m + z * n, z * m + y * n, x
        return x, z * m + y * n, y * m + z * n

    def coords(p, p1, p2, p3):
        m, n = yz[p]
        if p == 0:
            return p3, p1 * m + p2 * n, p2 * m + p1 * n
        return p1, p3 * m + p2 * n, p2 * m + p3 * n

    def peer(p, d1, d2, d3):
        p1, p2, p3 = pos(p)
        return device(*coords(p, (p1 + d1) % 4, (p2 + d2) % 4, (p3 + d3) % 4), c)

    def wslot(p, a3, a2_, start, n):
        if p == 0:
            return wgp.at[a2_, pl.ds(start, n), a3]
        bx, by, bz = coords(p, 0, a2_, a3)
        if p == 1:
            return wgn.at[bz % 2, by, bz // 2, pl.ds(start, n)]
        return wgn.at[2, by, bz // 2, pl.ds(start, n), :, pl.ds(pl.multiple_of((bz % 2) * 128, 128), 128)]

    def remote(src, dst, ss, rs, dev):
        return pltpu.make_async_remote_copy(
            src_ref=src, dst_ref=dst, send_sem=ss, recv_sem=rs, device_id=dev, device_id_type=MESH
        )

    mine = pl.ds(pl.multiple_of(c * HC, 128), HC)
    theirs = pl.ds(pl.multiple_of((1 - c) * HC, 128), HC)
    loads = [
        pltpu.make_async_copy(a_hbm, a2.at[0], loc.at[0]),
        pltpu.make_async_copy(t_hbm.at[:, mine], t2.at[0], loc.at[1]),
        pltpu.make_async_copy(r_hbm.at[:, mine], r2.at[0], loc.at[2]),
    ]
    for copy in loads:
        copy.start()

    partners = [sib, device(x, y, z + 1 - 2 * zl, 1 - c)]
    for d in (1, 2, 3):
        partners.append(device((x + d) % 4, y, z, c))
        partners.append(device(x, (y + d) % 4, z, c))
        partners.append(device(x, y, (z + d) % 4, c))
    barrier = pltpu.get_barrier_semaphore()
    for q in partners:
        pl.semaphore_signal(barrier, inc=1, device_id=q, device_id_type=MESH)

    lane = lax.broadcasted_iota(jnp.int32, (1, CAP), 1)
    live = lane < cnt_ref[0]
    weight = jnp.where(live, lw_ref[...], 0).astype(F32)
    magnitude = jnp.sum(jnp.abs(weight), axis=1, keepdims=True)
    rows8 = lax.broadcasted_iota(jnp.int32, (8, CAP), 0)
    meta[0] = jnp.where(
        rows8 == 0,
        jnp.broadcast_to(ref_ref[...], (8, CAP)),
        jnp.where(
            rows8 == 1,
            jnp.broadcast_to(weight, (8, CAP)),
            jnp.where(
                rows8 == 2,
                jnp.broadcast_to(seg_ref[...].astype(F32), (8, CAP)),
                jnp.broadcast_to(magnitude, (8, CAP)),
            ),
        ),
    )

    def shard_columns(core):
        base = core * HC
        return jnp.concatenate(
            [
                w_ref[:, pl.ds(pl.multiple_of(base + zl * 256, 128), 256)].astype(F32),
                w_ref[:, pl.ds(pl.multiple_of(base + 512 + zl * 256, 128), 256)].astype(F32),
                w_ref[:, pl.ds(pl.multiple_of(base + 1024 + zl * 128, 128), 128)].astype(F32),
            ],
            axis=1,
        )

    wx[0] = shard_columns(1 - c)
    gain_row[0, :] = gain_in[...]
    pl.semaphore_wait(barrier, len(partners))

    sib_w = remote(wx.at[0], wx.at[1], sib_s.at[0], sib_r.at[0], sib)
    sib_m = remote(meta.at[0], meta.at[1], sib_s.at[1], sib_r.at[1], sib)
    sib_a = remote(a_hbm, a2.at[1], sib_s.at[2], sib_r.at[2], sib)
    sib_t = remote(t_hbm.at[:, theirs], t2.at[1], sib_s.at[3], sib_r.at[3], sib)
    sib_res = remote(r_hbm.at[:, theirs], r2.at[1], sib_s.at[4], sib_r.at[4], sib)
    for copy in (sib_w, sib_m, sib_a, sib_t, sib_res):
        copy.start()

    own_w = shard_columns(c)
    sib_w.wait_recv()
    got_w = wx[1]
    first = c == 0
    block = jnp.concatenate(
        [jnp.where(first, own_w, got_w), jnp.where(first, got_w, own_w)], axis=0
    ).astype(BF16)
    bx0, by0, bz0 = x, y, z // 2
    wgp[pos(0)[1], pos(0)[0], x] = block[:, 0:256]
    wgn[zl, by0, bz0, bx0] = block[:, 256:512]
    wgn[2, by0, bz0, bx0, :, pl.ds(pl.multiple_of(zl * 128, 128), 128)] = block[:, 512:640]

    ph1, ph2, ph3, ph4 = {}, {}, {}, {}
    for p in pieces:
        p1, p2, p3 = pos(p)
        for d in (1, 2, 3):
            slot = wslot(p, p3, p2, p1, 1)
            ph1[p, d] = remote(slot, slot, p1_s.at[p, d - 1], p1_r.at[p, d - 1], peer(p, d, 0, 0))
            line = wslot(p, p3, p2, 0, 4)
            ph2[p, d] = remote(line, line, p2_s.at[p, d - 1], p2_r.at[p, d - 1], peer(p, 0, d, 0))
        for d in range(4):
            a2_ = (p2 + d) % 4
            line = wslot(p, p3, a2_, 0, 4)
            low = wslot(p, (p3 + 3) % 4, a2_, 0, 2)
            high = wslot(p, (p3 + 1) % 4, a2_, 2, 2)
            ph3[p, d, 0] = remote(line, line, p3_s.at[p, d, 0], p3_r.at[p, d, 0], peer(p, 0, 0, 1))
            ph3[p, d, 1] = remote(line, line, p3_s.at[p, d, 1], p3_r.at[p, d, 1], peer(p, 0, 0, 3))
            ph4[p, d, 0] = remote(low, low, p4_s.at[p, d, 0], p4_r.at[p, d, 0], peer(p, 0, 0, 1))
            ph4[p, d, 1] = remote(high, high, p4_s.at[p, d, 1], p4_r.at[p, d, 1], peer(p, 0, 0, 3))

    sends = [sib_w, sib_m, sib_a, sib_t, sib_res]

    def start(copy):
        copy.start()
        sends.append(copy)

    for d in (1, 3, 2):
        for p in pieces:
            start(ph1[p, d])

    def den_phase(axis, value):
        at_ = (x, y, z)[axis]
        den[axis, at_] = value
        copies = []
        for d in (1, 2, 3):
            q = [x, y, z]
            q[axis] = (at_ + d) % 4
            slot = den.at[axis, at_]
            copy = remote(
                slot, slot, den_s.at[axis, d - 1], den_r.at[axis, d - 1], device(q[0], q[1], q[2], c)
            )
            start(copy)
            copies.append(copy)
        return copies

    def den_total(axis, copies):
        for copy in copies:
            copy.wait_recv()
        return den[axis, 0] + den[axis, 1] + den[axis, 2] + den[axis, 3]

    sib_m.wait_recv()
    den_copies = den_phase(0, meta[0, :, 0:128] * 0 + (meta[0, 3:4, 0:128] + meta[1, 3:4, 0:128]))

    def transpose_rows(slot):
        @pl.loop(0, DW // 128)
        def _(k):
            off = pl.ds(pl.multiple_of(k * 128, 128), 128)
            at[off, slot * CAP : (slot + 1) * CAP] = a2[slot, :, off].T

    def transpose_targets(slot):
        @pl.loop(0, NG)
        def _(g):
            for k in (0, 1):
                off = pl.ds(pl.multiple_of(g * GW + k * 128, 128), 128)
                tt[g, k * 128 : (k + 1) * 128, slot * CAP : (slot + 1) * CAP] = t2[slot, :, off].T

    def slabs(p, v, h):
        m, n = yz[p]
        rows, weights = [], []
        if p == 0:
            for yy in range(4):
                for zz in range(2):
                    zc = 2 * zz + h
                    rows.append(at[pl.ds(pl.multiple_of(((yy * 2 + zz) * 4 + v) * ROW, 16), ROW), :])
                    weights.append(wgp[zc * m + yy * n, yy * m + zc * n, v])
            side = h
        else:
            side = h * m + (v % 2) * n
            for k in (0, 1):
                by = v * m + (2 * k + h) * n
                bz = k * m + (v // 2) * n
                rows.append(at[pl.ds(pl.multiple_of((by * 2 + bz) * 4 * ROW, 16), 4 * ROW), :])
                if p == 1:
                    weights.append(wgn[side, by, bz].reshape(4 * ROW, GW))
                else:
                    part = wgn[2, by, bz, :, :, pl.ds(pl.multiple_of(side * 128, 128), 128)]
                    weights.append(part.reshape(4 * ROW, 128))
        return jnp.concatenate(rows, axis=0), jnp.concatenate(weights, axis=0), side

    def forward(p, v):
        @pl.loop(0, 2)
        def _(h):
            rows, weights, side = slabs(p, v, h)
            res = lax.dot_general(weights, rows, (((0,), (0,)), ((), ())), preferred_element_type=F32)
            if p == 0:
                pr[side] += res
            elif p == 1:
                pr[2 + side] += res
            else:
                pr[4, pl.ds(pl.multiple_of(side * 128, 128), 128)] += res

    def last_place(p, d):
        return (pos(p)[2] + d) % 4

    gcol[...] = jnp.broadcast_to(
        gain_row[:, pl.ds(pl.multiple_of(c * HC, 128), HC)], (128, HC)
    ).T.reshape(NG, GW, 128)

    @pl.loop(0, NG)
    def _(g):
        pr[g] = jnp.zeros((GW, 2 * CAP), F32)

    for copy in loads:
        copy.wait()

    for p in pieces:
        for d in (1, 3, 2):
            ph1[p, d].wait_recv()
        for d in (1, 3, 2):
            start(ph2[p, d])
        if p == 0:
            start(ph3[p, 0, 0])
            start(ph3[p, 0, 1])
    for p in (1, 2):
        start(ph3[p, 0, 0])
        start(ph3[p, 0, 1])
    den_copies = den_phase(1, den_total(0, den_copies))

    def spread(p, d):
        ph2[p, 4 - d].wait_recv()
        start(ph3[p, d, 0])
        start(ph3[p, d, 1])

    def relay(p, d):
        for s in (0, 1):
            ph3[p, d, s].wait_recv()
            start(ph4[p, d, s])

    for d in (1, 3, 2):
        spread(0, d)
    transpose_rows(0)
    relay(0, 0)
    den_copies = den_phase(2, den_total(1, den_copies))
    sib_a.wait_recv()
    transpose_rows(1)
    for d in (1, 3, 2):
        spread(1, d)
        spread(2, d)
    relay(0, 1)
    forward(0, last_place(0, 0))
    sib_t.wait_recv()
    sib_res.wait_recv()
    for slot in (0, 1):
        part = jnp.zeros((CAP, 128), F32)
        for k in range(HC // 128):
            cols = slice(k * 128, (k + 1) * 128)
            part += t2[slot, :, cols].astype(F32) * r2[slot, :, cols].astype(F32)
        sp[0, slot] = jnp.broadcast_to(jnp.sum(part.T, axis=0, keepdims=True), (8, CAP))
    relay(1, 0)
    relay(2, 0)
    relay(0, 3)
    transpose_targets(0)
    forward(1, last_place(1, 0))
    forward(2, last_place(2, 0))
    relay(1, 1)
    relay(2, 1)
    relay(0, 2)
    transpose_targets(1)
    forward(0, last_place(0, 1))
    forward(0, last_place(0, 3))
    for d in (3, 2):
        relay(1, d)
        relay(2, d)
    for p in (1, 2):
        for d in (1, 3):
            forward(p, last_place(p, d))
    denominator = jnp.maximum(den_total(2, den_copies)[0:1, 0:1], 1.0)
    for p in pieces:
        for d in ORDER:
            for s in (0, 1):
                ph4[p, d, s].wait_recv()
        forward(p, last_place(p, 2))

    stat[...] = jnp.zeros((2, 8, 2 * CAP), F32)

    @pl.loop(0, NG)
    def _(g):
        for slot in (0, 1):
            cols = slice(slot * CAP, (slot + 1) * CAP)
            gains = jnp.concatenate([gcol[g]] * 4, axis=1)
            p_ = pr[g, :, cols]
            stat[0, :, cols] += jnp.sum((p_ * p_).reshape(GW // 8, 8, CAP), axis=0)
            tp = p_ * tt[g, :, cols].astype(F32) * gains
            stat[1, :, cols] += jnp.sum(tp.reshape(GW // 8, 8, CAP), axis=0)

    row = lax.broadcasted_iota(jnp.int32, (8, CAP), 0)
    for slot in (0, 1):
        cols = slice(slot * CAP, (slot + 1) * CAP)
        q1 = jnp.sum(stat[0, :, cols], axis=0, keepdims=True)
        q3 = jnp.sum(stat[1, :, cols], axis=0, keepdims=True)
        sp[0, slot] = jnp.where(row == 0, q1, jnp.where(row == 1, q3, sp[0, slot]))

    swap = [
        remote(sp.at[0, s], sp.at[1, 1 - s], sib_s.at[5 + s], sib_r.at[5 + s], sib) for s in (0, 1)
    ]
    for copy in swap:
        start(copy)
    for copy in swap:
        copy.wait_recv()

    segs = lax.broadcasted_iota(jnp.int32, (SEGS, CAP), 0).astype(F32)
    gsum[0, x] = jnp.zeros((8, HC + 128), F32)
    for slot in (0, 1):
        total = sp[0, slot] + sp[1, slot]
        q1, q3, q2 = total[0:1], total[1:2], total[2:3]
        scale = jnp.sqrt(q1 * (1.0 / DW) + 1e-06)
        score = q2 + q3 / scale
        ref, wgt, seg = meta[slot, 0:1], meta[slot, 1:2], meta[slot, 2:3]
        forget = jnp.maximum(-wgt, 0.0)
        retain = jnp.maximum(wgt, 0.0)
        table = (seg == segs).astype(F32)
        seg_sum = jnp.sum(table * (forget * (score - ref)), axis=1, keepdims=True)
        has = jnp.sum(table * forget, axis=1, keepdims=True) > 0.5
        scaled = npo_beta * seg_sum
        if slot == 0:
            soft = jnp.maximum(scaled, 0.0) + jnp.log1p(jnp.exp(-jnp.abs(scaled)))
            npo = jnp.sum(jnp.where(has, 2.0 / npo_beta * soft, 0.0), axis=0, keepdims=True)
            loss = npo - jnp.sum(retain * score, axis=1, keepdims=True)
            gsum[0, x, 0:1, HC : HC + 128] = jnp.broadcast_to(loss, (1, 128))
        sig = jnp.sum(table * jax.nn.sigmoid(scaled), axis=0, keepdims=True)
        grad = loss_scale / denominator * (forget * 2.0 * sig - retain)
        alpha[slot] = jnp.broadcast_to(grad / scale, (8, CAP))
        beta[slot] = jnp.broadcast_to(q3 / (scale * scale * DW), (8, CAP))

    @pl.loop(0, NG)
    def _(g):
        gains = jnp.concatenate([gcol[g]] * 4, axis=1)
        part = jnp.zeros((GW, 128), F32)
        for slot in (0, 1):
            cols = slice(slot * CAP, (slot + 1) * CAP)
            al, be = alpha[slot, 0:1], beta[slot, 0:1]
            p_ = pr[g, :, cols]
            t = tt[g, :, cols].astype(F32)
            pg[g, :, cols] = (al * (t * gains - p_ * be)).astype(BF16)
            u = al * t * p_
            part += (u[:, 0:128] + u[:, 128:256]) + (u[:, 256:384] + u[:, 384:512])
        gacc[g] = part

    @pl.loop(0, NG)
    def _(g):
        cols = pl.ds(pl.multiple_of(g * GW, GW), GW)
        gsum[0, x, 0:1, cols] = jnp.sum(gacc[g].T, axis=0, keepdims=True)

    def grad_blocks(p, v, emit):
        m, n = yz[p]
        for h in (0, 1):
            rows, _, side = slabs(p, v, h)
            if p == 2:
                right = pg[4, pl.ds(pl.multiple_of(side * 128, 128), 128)]
            else:
                right = pg[2 * p + side]
            res = lax.dot_general(rows, right, (((1,), (1,)), ((), ())), preferred_element_type=F32)
            for k in range(8):
                value = res[k * ROW : (k + 1) * ROW]
                if p == 0:
                    yy, zc = k // 2, 2 * (k % 2) + h
                    emit(zc * m + yy * n, yy * m + zc * n, value)
                else:
                    emit(2 * (k // 4) + h, k % 4, value)

    q0, qa, q1, q2, q3 = {}, {}, {}, {}, {}
    for p in pieces:
        p1, p2, p3 = pos(p)
        for s in (0, 1):
            half = pl.ds(2 * s, 2)
            to = peer(p, 0, 0, 1 + 2 * s)
            q0[p, s] = remote(st_o[p].at[:, half], rl[p].at[s], q0_s.at[p, s], q0_r.at[p, s], to)
            free = pl.ds(2 * (1 - s), 2)
            qa[p, s] = remote(
                st_n[p].at[s, :, free], rv[p].at[s, :, free], qa_s.at[p, s], qa_r.at[p, s], to
            )
            for d in range(4):
                i = (p2 + d) % 4
                q1[p, s, d] = remote(
                    st_n[p].at[s, i, half], rv[p].at[s, i, half], q1_s.at[p, s, d], q1_r.at[p, s, d], to
                )
        for d in (1, 2, 3):
            q2[p, d] = remote(
                s2[p].at[d - 1], v2[p].at[d - 1], q2_s.at[p, d - 1], q2_r.at[p, d - 1], peer(p, 0, d, 0)
            )
            q3[p, d] = remote(
                s3[p].at[d - 1], v3[p].at[d - 1], q3_s.at[p, d - 1], q3_r.at[p, d - 1], peer(p, d, 0, 0)
            )

    def put(ref, prefix=()):
        def emit(i, j, value):
            ref[prefix + (i, j)] = value.astype(ref.dtype)

        return emit

    for p in pieces:
        grad_blocks(p, (pos(p)[2] + 2) % 4, put(st_o[p]))
        start(q0[p, 0])
        start(q0[p, 1])

    def gain_phase(axis):
        at_ = (x, y, z)[axis]
        copies = []
        for d in (1, 2, 3):
            q = [x, y, z]
            q[axis] = (at_ + d) % 4
            slot = gsum.at[axis, at_]
            copy = remote(
                slot, slot, g_s.at[axis, d - 1], g_r.at[axis, d - 1], device(q[0], q[1], q[2], c)
            )
            start(copy)
            copies.append(copy)
        return copies

    def gain_total(axis, copies):
        for copy in copies:
            copy.wait_recv()
        return (gsum[axis, 0] + gsum[axis, 1]) + (gsum[axis, 2] + gsum[axis, 3])

    gain_copies = gain_phase(0)

    for p in pieces:
        for t_ in (0, 1):
            grad_blocks(p, (pos(p)[2] + 1 + 2 * t_) % 4, put(st_n[p], (t_,)))
            start(qa[p, t_])

    gsum[1, y] = gain_total(0, gain_copies)
    gain_copies = gain_phase(1)

    for p in pieces:
        grad_blocks(p, pos(p)[2], put(own[p]))

    for p in (1, 2, 0):
        for d in (2, 1, 3, 0):
            i = (pos(p)[1] + d) % 4
            for t_ in (0, 1):
                if d == 2:
                    q0[p, t_].wait_recv()
                half = slice(2 * t_, 2 * t_ + 2)
                both = st_n[p][t_, i, half].astype(F32) + rl[p][t_, i].astype(F32)
                st_n[p][t_, i, half] = both.astype(BF16)
                start(q1[p, t_, d])

    gsum[2, z] = gain_total(1, gain_copies)
    gain_copies = gain_phase(2)

    def lines(h, yy):
        m, n = yz[0]
        out = []
        for zz in range(2):
            zc = 2 * zz + h
            out.append(wgp[zc * m + yy * n, yy * m + zc * n].reshape(4 * ROW, GW))
        return jnp.concatenate(out, axis=0)

    def grad_rows(slot, yy):
        res = jnp.zeros((640, CAP), F32)
        for g in range(NG):
            w = lines(g, yy) if g < 2 else wgn[g - 2, yy].reshape(640, GW)
            right = pg[g, :, slot * CAP : (slot + 1) * CAP]
            res = res + jnp.dot(w, right, preferred_element_type=F32)
        return res

    @pl.loop(0, 4)
    def _(yy):
        ga_send[pl.ds(pl.multiple_of(yy * 640, 128), 640), :] = grad_rows(1, yy).astype(BF16)

    ga_copy = remote(ga_send, ga_recv, sib_s.at[7], sib_r.at[7], sib)
    start(ga_copy)

    def reduce_step(p, d):
        p1, p2, p3 = pos(p)
        i = (p2 + d) % 4
        for t_ in (0, 1):
            if d == 2:
                qa[p, t_].wait_recv()
            q1[p, t_, d].wait_recv()
        total = own[p][i] + rv[p][0, i].astype(F32) + rv[p][1, i].astype(F32)
        if d == 0:
            own[p][i] = total
        else:
            s2[p][d - 1] = total.astype(BF16)
            start(q2[p, d])

    reduce_step(1, 2)
    reduce_step(2, 2)
    reduce_step(1, 1)
    reduce_step(2, 1)

    ga_copy.wait_recv()

    @pl.loop(0, 4)
    def _(yy):
        rows = pl.ds(pl.multiple_of(yy * 640, 128), 640)
        both = (grad_rows(0, yy) + ga_recv[rows, :].astype(F32)).astype(BF16)
        for k in range(5):
            cols = pl.ds(pl.multiple_of(yy * 640 + k * 128, 128), 128)
            ga_own[:, cols] = both[k * 128 : (k + 1) * 128].T

    ga_store = pltpu.make_async_copy(ga_own, ga_out, loc.at[3])
    ga_store.start()

    for p, d in ((1, 3), (2, 3), (0, 2), (1, 0), (2, 0)):
        reduce_step(p, d)

    def second(p):
        p1, p2, p3 = pos(p)
        acc = own[p][p2]
        for d in (1, 3, 2):
            q2[p, d].wait_recv()
            acc = acc + v2[p][d - 1].astype(F32)
        own[p][p2] = acc
        for d in (1, 3, 2):
            s3[p][d - 1] = own[p][p2, (p1 + d) % 4].astype(BF16)
            start(q3[p, d])

    offs = (0, 256, 512)
    keep = pl.ds(pl.multiple_of(c * HALF, 8), HALF)
    give = pl.ds(pl.multiple_of((1 - c) * HALF, 8), HALF)
    zn = z + 1 - 2 * zl
    last = {}

    def third(p):
        p1, p2, p3 = pos(p)
        acc = own[p][p2, p1]
        for d in (1, 3, 2):
            q3[p, d].wait_recv()
            acc = acc + v3[p][d - 1].astype(F32)
        cols = slice(offs[p], offs[p] + WIDTH[p])
        fb[:, cols] = acc
        last[p] = [
            remote(fb.at[give, cols], fr.at[0, :, cols], qf_s.at[p, 0], qf_r.at[p, 0], sib),
            remote(fb.at[keep, cols], fr.at[1, :, cols], qf_s.at[p, 1], qf_r.at[p, 1], device(x, y, zn, c)),
            remote(fb.at[give, cols], fr.at[2, :, cols], qf_s.at[p, 2], qf_r.at[p, 2], device(x, y, zn, 1 - c)),
        ]
        for copy in (last[p][1], last[p][2], last[p][0]):
            start(copy)

    reduce_step(0, 1)
    second(1)
    second(2)
    reduce_step(0, 3)
    reduce_step(0, 0)
    second(0)

    total = gain_total(2, gain_copies)
    gsib[c] = total
    gcopy = remote(gsib.at[c], gsib.at[c], sib_s.at[8], sib_r.at[8], sib)
    start(gcopy)

    third(1)
    third(2)
    third(0)

    def place_columns(core, side, value):
        base = core * HC
        gw_out[:, pl.ds(pl.multiple_of(base + side * 256, 128), 256)] = value[:, 0:256]
        gw_out[:, pl.ds(pl.multiple_of(base + 512 + side * 256, 128), 256)] = value[:, 256:512]
        gw_out[:, pl.ds(pl.multiple_of(base + 1024 + side * 128, 128), 128)] = value[:, 512:640]

    place_columns(c, zl, fb[keep])

    gcopy.wait_recv()
    for core in (0, 1):
        gg_out[:, core * HC : (core + 1) * HC] = gsib[core, 0:1, 0:HC]
    loss_out[...] = (gsib[0, 0:1, HC : HC + 128] + gsib[1, 0:1, HC : HC + 128]) / denominator

    for p in (1, 2, 0):
        for copy in last[p]:
            copy.wait_recv()
    place_columns(1 - c, zl, fr[0])
    place_columns(c, 1 - zl, fr[1])
    place_columns(1 - c, 1 - zl, fr[2])

    for copy in sends:
        copy.wait_send()
    ga_store.wait()


def scratch():
    dma = pltpu.SemaphoreType.DMA
    vm = pltpu.VMEM
    out = [
        vm((1, DW), F32),
        vm((NG, GW, 128), F32),
        vm((2, CAP, DW), BF16),
        vm((DW, 2 * CAP), BF16),
        vm((2, CAP, HC), BF16),
        vm((2, CAP, HC), BF16),
        vm((NG, GW, 2 * CAP), BF16),
        vm((4, 4, 4, ROW, GW), BF16),
        vm((NG - 2, 4, 2, 4, ROW, GW), BF16),
        vm((NG, GW, 2 * CAP), F32),
        vm((NG, GW, 2 * CAP), BF16),
        vm((2, HALF, 640), F32),
        vm((2, 8, CAP), F32),
        vm((2, 8, 2 * CAP), F32),
        vm((2, 2, 8, CAP), F32),
        vm((2, 8, CAP), F32),
        vm((2, 8, CAP), F32),
        vm((NG, GW, 128), F32),
        vm((3, 4, 8, 128), F32),
        vm((3, 4, 8, HC + 128), F32),
        vm((2, 8, HC + 128), F32),
    ]
    out += [vm((4, 4, ROW, w), BF16) for w in WIDTH]
    out += [vm((2, 4, 4, ROW, w), BF16) for w in WIDTH]
    out += [vm((2, 4, 2, ROW, w), BF16) for w in WIDTH]
    out += [vm((2, 4, 4, ROW, w), BF16) for w in WIDTH]
    out += [vm((4, 4, ROW, w), F32) for w in WIDTH]
    out += [vm((3, 4, ROW, w), BF16) for w in WIDTH]
    out += [vm((3, 4, ROW, w), BF16) for w in WIDTH]
    out += [vm((3, ROW, w), BF16) for w in WIDTH]
    out += [vm((3, ROW, w), BF16) for w in WIDTH]
    out += [
        vm((ROW, 640), F32),
        vm((3, HALF, 640), F32),
        vm((DW, CAP), BF16),
        vm((DW, CAP), BF16),
        vm((CAP, DW), BF16),
        dma((4,)),
    ]
    for shape in ((9,), (3, 3), (3, 3), (3, 3), (3, 3), (3, 4, 2), (3, 4, 2), (3, 2), (3, 2), (3, 2, 4), (3, 3), (3, 3), (3, 3)):
        out += [dma(shape), dma(shape)]
    return out


def finish(gw, gg, ga, loss, gw_out, gg_out, ga_out, loss_out, gw_v, ga_v, s_in, s_out):
    n = CAP // PARTS
    pairs = [(gw, gw_v, gw_out)]
    for k in range(PARTS):
        rows = slice(k * n, (k + 1) * n)
        pairs.append((ga.at[rows], ga_v.at[rows], ga_out.at[rows]))
    loads = [pltpu.make_async_copy(src, mid, s_in.at[i]) for i, (src, mid, _) in enumerate(pairs)]
    stores = [pltpu.make_async_copy(mid, dst, s_out.at[i]) for i, (_, mid, dst) in enumerate(pairs)]
    for copy in loads:
        copy.start()
    gg_out[...] = gg[0, :]
    loss_out[0, 0] = loss[0, 0]
    for load, store in zip(loads, stores):
        load.wait()
        store.start()
    for copy in stores:
        copy.wait()


def shards(attention_out, residual, target_rows, ref_logit, loss_weight, segment, counts, out_weight, norm_gain):
    any_ = pl.BlockSpec(memory_space=pl.ANY)
    vmem = pl.BlockSpec(memory_space=pltpu.VMEM)
    smem = pl.BlockSpec(memory_space=pltpu.SMEM)
    gw, gg, ga, loss = pl.pallas_call(
        kernel,
        out_shape=(
            jax.ShapeDtypeStruct((HALF, DW), F32),
            jax.ShapeDtypeStruct((1, DW), F32),
            jax.ShapeDtypeStruct((CAP, DW), BF16),
            jax.ShapeDtypeStruct((1, 128), F32),
        ),
        in_specs=[any_, any_, any_, vmem, vmem, vmem, smem, vmem, vmem],
        out_specs=(vmem, vmem, any_, vmem),
        scratch_shapes=scratch(),
        compiler_params=pltpu.CompilerParams(
            collective_id=0, has_side_effects=True, vmem_limit_bytes=62 * 2**20
        ),
        cost_estimate=pl.CostEstimate(
            flops=3 * 2 * CAP * DW * DW, bytes_accessed=4 * CAP * DW * 2, transcendentals=0
        ),
    )(
        attention_out,
        residual,
        target_rows,
        ref_logit,
        loss_weight,
        segment,
        counts,
        out_weight,
        norm_gain,
    )
    gw, gg, ga, loss = pl.pallas_call(
        finish,
        out_shape=(
            jax.ShapeDtypeStruct((HALF, DW), F32),
            jax.ShapeDtypeStruct((DW,), F32),
            jax.ShapeDtypeStruct((CAP, DW), BF16),
            jax.ShapeDtypeStruct((1, 1), F32),
        ),
        in_specs=[any_, vmem, any_, vmem],
        out_specs=(any_, vmem, any_, smem),
        scratch_shapes=[
            pltpu.VMEM((HALF, DW), F32),
            pltpu.VMEM((CAP, DW), BF16),
            pltpu.SemaphoreType.DMA((PARTS + 1,)),
            pltpu.SemaphoreType.DMA((PARTS + 1,)),
        ],
        compiler_params=pltpu.CompilerParams(vmem_limit_bytes=62 * 2**20),
    )(gw, gg, ga, loss)
    return gw, gg, ga, loss[0, 0]


def solution(mesh):
    rows = P(("dp", "fsdp"), None)
    placed = (rows,) * 6 + (P(("dp", "fsdp")), P("fsdp", None), P())
    return jax.shard_map(
        shards,
        mesh=mesh,
        in_specs=placed,
        out_specs=(P("fsdp", None), P(), rows, P()),
        check_vma=False,
    )
```

time: 130 us -> 111 us (0.85)
  Pallas kernels: 119 us -> 109 us
  local copies, waits for them, and re-layouts: 6.5 us -> 0 us
  other arithmetic: 1.33 us -> 0 us
    pallas_call x1, Pallas kernels: 119 us -> 105 us  [shards(): pl.pallas_call(kernel, out_shape=(jax.ShapeDtypeStruct((HALF, DW), F32),...]
    unnamed x4 -> x0, local copies, waits for them, and re-layouts: 5.18 us -> none
    pallas_call x0 -> x1, Pallas kernels: none -> 4.08 us  [shards(): pl.pallas_call(finish, out_shape=(jax.ShapeDtypeStruct((HALF, DW), F32),...]
    pallas_call x1 -> x0, other arithmetic: 1.33 us -> none  [shards(): pl.pallas_call(kernel, out_shape=(jax.ShapeDtypeStruct((HALF, DW), F32),...]
    reshape x1 -> x0, local copies, waits for them, and re-layouts: 1.31 us -> none  [shards(): norm_gain.reshape(1, DW)]
where the time goes in v2:
time: 111 us; the launch traced here: 110 us
  Pallas kernels  109 us (98%)
  between operations  1.45 us (1%)
    pallas_call x1, Pallas kernels, shards(): pl.pallas_call(kernel, out_shape=(jax.ShapeDtypeStruct((HALF, DW), F32),...  105 us
    pallas_call x1, Pallas kernels, shards(): pl.pallas_call(finish, out_shape=(jax.ShapeDtypeStruct((HALF, DW), F32),...  4.08 us

profile of v2, /device:TPU:1, one launch (start us, length us, event | category | flops | bytes accessed | tf_op | source)
XLA Modules:
  0.0 110.3 jit_solution(14706096195120625296)
XLA Ops:
  1.3 104.8 %shard_map.120 = (f32[40,2560]{1,0:T(8,128)}, f32[1,2560]{1,0:T(1,128)}, bf16[512,2560]{1,0:T(8,128)(2,1)}, f32[1,128]{1,0:T(1,128)}) custom-call(bf16[512,2560]{1,0:T(8,128)(2,1)} %a_hbm.1, bf16[512,2560]{1,0:T(8,128)(2,1)} %r_hbm.1, bf16[512,2560]{1,0:T(8,128)(2,1)} %t_hbm.1, f32[1,512]{1,0:T(1,128)} %ref_ref.1, s32[1,512]{1,0:T(1,128)} %lw_ref.1, ...), custom_call_target="tpu_custom_call" | custom-call | flops 20132659200 | bytes 10485760 | tf_op jit(solution)/shard_map/pallas_call | solution.py:773
  106.1 4.1 %shard_map.121 = (f32[40,2560]{1,0:T(8,128)}, f32[2560]{0:T(1024)}, bf16[512,2560]{1,0:T(8,128)(2,1)}, f32[1,1]{1,0:T(1,128)}) custom-call(f32[40,2560]{1,0:T(8,128)} %get-tuple-element.12.gw, f32[1,2560]{1,0:T(1,128)} %get-tuple-element.13.gg, bf16[512,2560]{1,0:T(8,128)(2,1)} %get-tuple-element.14.ga, f32[1,128]{1,0:T(1,128)} %get-tuple-element.15.loss), custom_call_target="tpu_custom_call" | custom-call | tf_op jit(solution)/shard_map/pallas_call | solution.py:801

commit v3 on v2

--- a/solution.py
+++ b/solution.py
@@ -17,6 +17,7 @@
 
 ROW = 80
 HALF = 40
+PAD = 48
 CAP = 512
 DW = 2560
 HC = 1280
@@ -79,6 +80,7 @@
     ow0, ow1, ow2,
     s20, s21, s22,
     v20, v21, v22,
+    w20, w21, w22,
     s30, s31, s32,
     v30, v31, v32,
     fb,
@@ -100,6 +102,7 @@
     q2_s, q2_r,
     q3_s, q3_r,
     qf_s, qf_r,
+    ga_s, ga_r,
 ):
     st_o = (st_o0, st_o1, st_o2)
     st_n = (st_n0, st_n1, st_n2)
@@ -108,6 +111,7 @@
     own = (ow0, ow1, ow2)
     s2 = (s20, s21, s22)
     v2 = (v20, v21, v22)
+    w2 = (w20, w21, w22)
     s3 = (s30, s31, s32)
     v3 = (v30, v31, v32)
     x, y, z, c = place()
@@ -165,7 +169,7 @@
         pl.semaphore_signal(barrier, inc=1, device_id=q, device_id_type=MESH)
 
     lane = lax.broadcasted_iota(jnp.int32, (1, CAP), 1)
-    live = lane < cnt_ref[0]
+    live = lane < cnt_ref[...].reshape(1, 1)
     weight = jnp.where(live, lw_ref[...], 0).astype(F32)
     magnitude = jnp.sum(jnp.abs(weight), axis=1, keepdims=True)
     rows8 = lax.broadcasted_iota(jnp.int32, (8, CAP), 0)
@@ -218,14 +222,19 @@
     wgn[zl, by0, bz0, bx0] = block[:, 256:512]
     wgn[2, by0, bz0, bx0, :, pl.ds(pl.multiple_of(zl * 128, 128), 128)] = block[:, 512:640]
 
-    ph1, ph2, ph3, ph4 = {}, {}, {}, {}
+    ph1, ph2, ph2r, ph3, ph4 = {}, {}, {}, {}, {}
     for p in pieces:
         p1, p2, p3 = pos(p)
         for d in (1, 2, 3):
             slot = wslot(p, p3, p2, p1, 1)
             ph1[p, d] = remote(slot, slot, p1_s.at[p, d - 1], p1_r.at[p, d - 1], peer(p, d, 0, 0))
-            line = wslot(p, p3, p2, 0, 4)
-            ph2[p, d] = remote(line, line, p2_s.at[p, d - 1], p2_r.at[p, d - 1], peer(p, 0, d, 0))
+        line = wslot(p, p3, p2, 0, 4)
+        low = wslot(p, p3, (p2 + 3) % 4, 0, 2)
+        high = wslot(p, p3, (p2 + 1) % 4, 2, 2)
+        ph2[p, 1] = remote(line, line, p2_s.at[p, 0], p2_r.at[p, 0], peer(p, 0, 1, 0))
+        ph2[p, 3] = remote(line, line, p2_s.at[p, 1], p2_r.at[p, 1], peer(p, 0, 3, 0))
+        ph2r[p, 1] = remote(low, low, p2_s.at[p, 2], p2_r.at[p, 2], peer(p, 0, 1, 0))
+        ph2r[p, 3] = remote(high, high, p2_s.at[p, 3], p2_r.at[p, 3], peer(p, 0, 3, 0))
         for d in range(4):
             a2_ = (p2 + d) % 4
             line = wslot(p, p3, a2_, 0, 4)
@@ -241,10 +250,6 @@
     def start(copy):
         copy.start()
         sends.append(copy)
-
-    for d in (1, 3, 2):
-        for p in pieces:
-            start(ph1[p, d])
 
     def den_phase(axis, value):
         at_ = (x, y, z)[axis]
@@ -268,6 +273,9 @@
 
     sib_m.wait_recv()
     den_copies = den_phase(0, meta[0, :, 0:128] * 0 + (meta[0, 3:4, 0:128] + meta[1, 3:4, 0:128]))
+    for d in (1, 3, 2):
+        for p in pieces:
+            start(ph1[p, d])
 
     def transpose_rows(slot):
         @pl.loop(0, DW // 128)
@@ -305,8 +313,8 @@
                     weights.append(part.reshape(4 * ROW, 128))
         return jnp.concatenate(rows, axis=0), jnp.concatenate(weights, axis=0), side
 
-    def forward(p, v):
-        @pl.loop(0, 2)
+    def forward(p, v, only=None):
+        @pl.loop(0 if only is None else only, 2 if only is None else only + 1)
         def _(h):
             rows, weights, side = slabs(p, v, h)
             res = lax.dot_general(weights, rows, (((0,), (0,)), ((), ())), preferred_element_type=F32)
@@ -317,6 +325,9 @@
             else:
                 pr[4, pl.ds(pl.multiple_of(side * 128, 128), 128)] += res
 
+    def near(p, d, odd):
+        forward(p, last_place(p, d), (pos(p)[1] + odd) % 2)
+
     def last_place(p, d):
         return (pos(p)[2] + d) % 4
 
@@ -334,7 +345,9 @@
     for p in pieces:
         for d in (1, 3, 2):
             ph1[p, d].wait_recv()
-        for d in (1, 3, 2):
+        if p == 0:
+            den_copies = den_phase(1, den_total(0, den_copies))
+        for d in (1, 3):
             start(ph2[p, d])
         if p == 0:
             start(ph3[p, 0, 0])
@@ -342,10 +355,14 @@
     for p in (1, 2):
         start(ph3[p, 0, 0])
         start(ph3[p, 0, 1])
-    den_copies = den_phase(1, den_total(0, den_copies))
 
     def spread(p, d):
-        ph2[p, 4 - d].wait_recv()
+        if d == 2:
+            ph2r[p, 1].wait_recv()
+            ph2r[p, 3].wait_recv()
+        else:
+            ph2[p, 4 - d].wait_recv()
+            start(ph2r[p, 4 - d])
         start(ph3[p, d, 0])
         start(ph3[p, d, 1])
 
@@ -354,18 +371,23 @@
             ph3[p, d, s].wait_recv()
             start(ph4[p, d, s])
 
-    for d in (1, 3, 2):
-        spread(0, d)
+    spread(0, 1)
+    spread(0, 3)
     transpose_rows(0)
     relay(0, 0)
+    for d in (1, 3):
+        spread(1, d)
+        spread(2, d)
     den_copies = den_phase(2, den_total(1, den_copies))
     sib_a.wait_recv()
     transpose_rows(1)
-    for d in (1, 3, 2):
-        spread(1, d)
-        spread(2, d)
+    spread(0, 2)
     relay(0, 1)
+    relay(1, 0)
+    relay(2, 0)
     forward(0, last_place(0, 0))
+    spread(1, 2)
+    spread(2, 2)
     sib_t.wait_recv()
     sib_res.wait_recv()
     for slot in (0, 1):
@@ -374,30 +396,39 @@
             cols = slice(k * 128, (k + 1) * 128)
             part += t2[slot, :, cols].astype(F32) * r2[slot, :, cols].astype(F32)
         sp[0, slot] = jnp.broadcast_to(jnp.sum(part.T, axis=0, keepdims=True), (8, CAP))
-    relay(1, 0)
-    relay(2, 0)
     relay(0, 3)
-    transpose_targets(0)
     forward(1, last_place(1, 0))
-    forward(2, last_place(2, 0))
     relay(1, 1)
     relay(2, 1)
+    transpose_targets(0)
+    transpose_targets(1)
+    forward(2, last_place(2, 0))
+    relay(1, 3)
+    relay(2, 3)
+    near(1, 1, 1)
+    near(1, 3, 1)
     relay(0, 2)
-    transpose_targets(1)
     forward(0, last_place(0, 1))
+    relay(1, 2)
+    relay(2, 2)
     forward(0, last_place(0, 3))
-    for d in (3, 2):
-        relay(1, d)
-        relay(2, d)
+    near(2, 1, 1)
+    near(2, 3, 1)
     for p in (1, 2):
-        for d in (1, 3):
-            forward(p, last_place(p, d))
+        near(p, 1, 0)
+        near(p, 3, 0)
     denominator = jnp.maximum(den_total(2, den_copies)[0:1, 0:1], 1.0)
-    for p in pieces:
-        for d in ORDER:
+    def arrived(p, steps):
+        for d in steps:
             for s in (0, 1):
                 ph4[p, d, s].wait_recv()
-        forward(p, last_place(p, 2))
+
+    arrived(0, ORDER)
+    forward(0, last_place(0, 2))
+    for odd in (1, 0):
+        for p in (1, 2):
+            arrived(p, (1, 3) if odd else (0, 2))
+            near(p, 2, odd)
 
     stat[...] = jnp.zeros((2, 8, 2 * CAP), F32)
 
@@ -427,7 +458,6 @@
         copy.wait_recv()
 
     segs = lax.broadcasted_iota(jnp.int32, (SEGS, CAP), 0).astype(F32)
-    gsum[0, x] = jnp.zeros((8, HC + 128), F32)
     for slot in (0, 1):
         total = sp[0, slot] + sp[1, slot]
         q1, q3, q2 = total[0:1], total[1:2], total[2:3]
@@ -486,7 +516,7 @@
                 else:
                     emit(2 * (k // 4) + h, k % 4, value)
 
-    q0, qa, q1, q2, q3 = {}, {}, {}, {}, {}
+    q0, qa, q1, q2, q2r, q3 = {}, {}, {}, {}, {}, {}
     for p in pieces:
         p1, p2, p3 = pos(p)
         for s in (0, 1):
@@ -502,10 +532,15 @@
                 q1[p, s, d] = remote(
                     st_n[p].at[s, i, half], rv[p].at[s, i, half], q1_s.at[p, s, d], q1_r.at[p, s, d], to
                 )
+        for t_ in (0, 1):
+            to = peer(p, 0, 1 + 2 * t_, 0)
+            q2[p, 1 + 2 * t_] = remote(
+                s2[p].at[2 * t_], v2[p].at[t_], q2_s.at[p, t_], q2_r.at[p, t_], to
+            )
+            q2r[p, t_] = remote(
+                s2[p].at[1, pl.ds(2 * t_, 2)], w2[p].at[t_], q2_s.at[p, 2 + t_], q2_r.at[p, 2 + t_], to
+            )
         for d in (1, 2, 3):
-            q2[p, d] = remote(
-                s2[p].at[d - 1], v2[p].at[d - 1], q2_s.at[p, d - 1], q2_r.at[p, d - 1], peer(p, 0, d, 0)
-            )
             q3[p, d] = remote(
                 s3[p].at[d - 1], v3[p].at[d - 1], q3_s.at[p, d - 1], q3_r.at[p, d - 1], peer(p, d, 0, 0)
             )
@@ -515,11 +550,6 @@
             ref[prefix + (i, j)] = value.astype(ref.dtype)
 
         return emit
-
-    for p in pieces:
-        grad_blocks(p, (pos(p)[2] + 2) % 4, put(st_o[p]))
-        start(q0[p, 0])
-        start(q0[p, 1])
 
     def gain_phase(axis):
         at_ = (x, y, z)[axis]
@@ -542,18 +572,17 @@
 
     gain_copies = gain_phase(0)
 
-    for p in pieces:
+    for p in (1, 2, 0):
+        grad_blocks(p, (pos(p)[2] + 2) % 4, put(st_o[p]))
+        start(q0[p, 0])
+        start(q0[p, 1])
+
+    for p in (1, 2, 0):
         for t_ in (0, 1):
             grad_blocks(p, (pos(p)[2] + 1 + 2 * t_) % 4, put(st_n[p], (t_,)))
             start(qa[p, t_])
 
-    gsum[1, y] = gain_total(0, gain_copies)
-    gain_copies = gain_phase(1)
-
-    for p in pieces:
-        grad_blocks(p, pos(p)[2], put(own[p]))
-
-    for p in (1, 2, 0):
+    def relay_sums(p):
         for d in (2, 1, 3, 0):
             i = (pos(p)[1] + d) % 4
             for t_ in (0, 1):
@@ -564,8 +593,15 @@
                 st_n[p][t_, i, half] = both.astype(BF16)
                 start(q1[p, t_, d])
 
-    gsum[2, z] = gain_total(1, gain_copies)
-    gain_copies = gain_phase(2)
+    for p in (1, 2):
+        grad_blocks(p, pos(p)[2], put(own[p]))
+    relay_sums(1)
+    relay_sums(2)
+    grad_blocks(0, pos(0)[2], put(own[0]))
+    relay_sums(0)
+
+    gsum[1, y] = gain_total(0, gain_copies)
+    gain_copies = gain_phase(1)
 
     def lines(h, yy):
         m, n = yz[0]
@@ -583,12 +619,26 @@
             res = res + jnp.dot(w, right, preferred_element_type=F32)
         return res
 
-    @pl.loop(0, 4)
-    def _(yy):
-        ga_send[pl.ds(pl.multiple_of(yy * 640, 128), 640), :] = grad_rows(1, yy).astype(BF16)
-
-    ga_copy = remote(ga_send, ga_recv, sib_s.at[7], sib_r.at[7], sib)
-    start(ga_copy)
+    ga_copies = []
+
+    def sibling_rows(yy):
+        rows = slice(yy * 640, (yy + 1) * 640)
+        ga_send[rows, :] = grad_rows(1, yy).astype(BF16)
+        copy = remote(ga_send.at[rows], ga_recv.at[rows], ga_s.at[yy], ga_r.at[yy], sib)
+        start(copy)
+        ga_copies.append(copy)
+
+    ga_stores = []
+
+    def own_rows(yy):
+        ga_copies[yy].wait_recv()
+        rows = slice(yy * 640, (yy + 1) * 640)
+        both = (grad_rows(0, yy) + ga_recv[rows, :].astype(F32)).astype(BF16)
+        for k in range(5):
+            ga_own[:, yy * 640 + k * 128 : yy * 640 + (k + 1) * 128] = both[k * 128 : (k + 1) * 128].T
+        copy = pltpu.make_async_copy(ga_own.at[:, rows], ga_out.at[:, rows], loc.at[3 + yy])
+        copy.start()
+        ga_stores.append(copy)
 
     def reduce_step(p, d):
         p1, p2, p3 = pos(p)
@@ -600,45 +650,30 @@
         total = own[p][i] + rv[p][0, i].astype(F32) + rv[p][1, i].astype(F32)
         if d == 0:
             own[p][i] = total
-        else:
-            s2[p][d - 1] = total.astype(BF16)
-            start(q2[p, d])
-
-    reduce_step(1, 2)
-    reduce_step(2, 2)
-    reduce_step(1, 1)
-    reduce_step(2, 1)
-
-    ga_copy.wait_recv()
-
-    @pl.loop(0, 4)
-    def _(yy):
-        rows = pl.ds(pl.multiple_of(yy * 640, 128), 640)
-        both = (grad_rows(0, yy) + ga_recv[rows, :].astype(F32)).astype(BF16)
-        for k in range(5):
-            cols = pl.ds(pl.multiple_of(yy * 640 + k * 128, 128), 128)
-            ga_own[:, cols] = both[k * 128 : (k + 1) * 128].T
-
-    ga_store = pltpu.make_async_copy(ga_own, ga_out, loc.at[3])
-    ga_store.start()
-
-    for p, d in ((1, 3), (2, 3), (0, 2), (1, 0), (2, 0)):
-        reduce_step(p, d)
+            return
+        s2[p][d - 1] = total.astype(BF16)
+        if d == 2:
+            start(q2r[p, 0])
+            start(q2r[p, 1])
+            return
+        t_ = d // 2
+        half = slice(2 * t_, 2 * t_ + 2)
+        q2r[p, t_].wait_recv()
+        s2[p][d - 1, half] = (total[half] + w2[p][t_].astype(F32)).astype(BF16)
+        start(q2[p, d])
 
     def second(p):
         p1, p2, p3 = pos(p)
         acc = own[p][p2]
-        for d in (1, 3, 2):
-            q2[p, d].wait_recv()
-            acc = acc + v2[p][d - 1].astype(F32)
+        for t_ in (0, 1):
+            q2[p, 1 + 2 * t_].wait_recv()
+            acc = acc + v2[p][t_].astype(F32)
         own[p][p2] = acc
         for d in (1, 3, 2):
             s3[p][d - 1] = own[p][p2, (p1 + d) % 4].astype(BF16)
             start(q3[p, d])
 
     offs = (0, 256, 512)
-    keep = pl.ds(pl.multiple_of(c * HALF, 8), HALF)
-    give = pl.ds(pl.multiple_of((1 - c) * HALF, 8), HALF)
     zn = z + 1 - 2 * zl
     last = {}
 
@@ -649,43 +684,67 @@
             q3[p, d].wait_recv()
             acc = acc + v3[p][d - 1].astype(F32)
         cols = slice(offs[p], offs[p] + WIDTH[p])
-        fb[:, cols] = acc
+        pad = jnp.zeros((PAD - HALF, WIDTH[p]), F32)
+        for core in (0, 1):
+            part = acc[core * HALF : (core + 1) * HALF]
+            fb[core, :, cols] = jnp.concatenate([part, pad], axis=0).astype(BF16)
+        mine_ = fb.at[c, :, cols]
+        other = fb.at[1 - c, :, cols]
         last[p] = [
-            remote(fb.at[give, cols], fr.at[0, :, cols], qf_s.at[p, 0], qf_r.at[p, 0], sib),
-            remote(fb.at[keep, cols], fr.at[1, :, cols], qf_s.at[p, 1], qf_r.at[p, 1], device(x, y, zn, c)),
-            remote(fb.at[give, cols], fr.at[2, :, cols], qf_s.at[p, 2], qf_r.at[p, 2], device(x, y, zn, 1 - c)),
+            remote(other, fr.at[0, :, cols], qf_s.at[p, 0], qf_r.at[p, 0], sib),
+            remote(mine_, fr.at[1, :, cols], qf_s.at[p, 1], qf_r.at[p, 1], device(x, y, zn, c)),
+            remote(other, fr.at[2, :, cols], qf_s.at[p, 2], qf_r.at[p, 2], device(x, y, zn, 1 - c)),
         ]
         for copy in (last[p][1], last[p][2], last[p][0]):
             start(copy)
 
+    sibling_rows(0)
+    sibling_rows(1)
+    sibling_rows(2)
+    sibling_rows(3)
+    reduce_step(1, 2)
+    reduce_step(2, 2)
+    own_rows(0)
+    own_rows(1)
+    reduce_step(0, 2)
+    reduce_step(1, 1)
+    reduce_step(2, 1)
+    reduce_step(1, 3)
+    reduce_step(2, 3)
+    gsum[2, z] = gain_total(1, gain_copies)
+    gain_copies = gain_phase(2)
     reduce_step(0, 1)
+    reduce_step(0, 3)
+    reduce_step(1, 0)
+    reduce_step(2, 0)
+    reduce_step(0, 0)
     second(1)
     second(2)
-    reduce_step(0, 3)
-    reduce_step(0, 0)
     second(0)
+    third(1)
+    third(2)
 
     total = gain_total(2, gain_copies)
     gsib[c] = total
     gcopy = remote(gsib.at[c], gsib.at[c], sib_s.at[8], sib_r.at[8], sib)
     start(gcopy)
 
-    third(1)
-    third(2)
     third(0)
+    own_rows(2)
+    own_rows(3)
 
     def place_columns(core, side, value):
         base = core * HC
+        value = value.astype(F32)[0:HALF]
         gw_out[:, pl.ds(pl.multiple_of(base + side * 256, 128), 256)] = value[:, 0:256]
         gw_out[:, pl.ds(pl.multiple_of(base + 512 + side * 256, 128), 256)] = value[:, 256:512]
         gw_out[:, pl.ds(pl.multiple_of(base + 1024 + side * 128, 128), 128)] = value[:, 512:640]
 
-    place_columns(c, zl, fb[keep])
+    place_columns(c, zl, fb[c])
 
     gcopy.wait_recv()
-    for core in (0, 1):
-        gg_out[:, core * HC : (core + 1) * HC] = gsib[core, 0:1, 0:HC]
-    loss_out[...] = (gsib[0, 0:1, HC : HC + 128] + gsib[1, 0:1, HC : HC + 128]) / denominator
+    gg_out[...] = jnp.concatenate([gsib[0, 0, 0:HC], gsib[1, 0, 0:HC]], axis=0)
+    loss_out[...] = (gsib[0, 0:1, HC : HC + 1] + gsib[1, 0:1, HC : HC + 1]) / denominator
 
     for p in (1, 2, 0):
         for copy in last[p]:
@@ -696,7 +755,8 @@
 
     for copy in sends:
         copy.wait_send()
-    ga_store.wait()
+    for copy in ga_stores:
+        copy.wait()
 
 
 def scratch():
@@ -722,8 +782,8 @@
         vm((2, 8, CAP), F32),
         vm((NG, GW, 128), F32),
         vm((3, 4, 8, 128), F32),
-        vm((3, 4, 8, HC + 128), F32),
-        vm((2, 8, HC + 128), F32),
+        vm((3, 4, 1, HC + 128), F32),
+        vm((2, 1, HC + 128), F32),
     ]
     out += [vm((4, 4, ROW, w), BF16) for w in WIDTH]
     out += [vm((2, 4, 4, ROW, w), BF16) for w in WIDTH]
@@ -731,34 +791,37 @@
     out += [vm((2, 4, 4, ROW, w), BF16) for w in WIDTH]
     out += [vm((4, 4, ROW, w), F32) for w in WIDTH]
     out += [vm((3, 4, ROW, w), BF16) for w in WIDTH]
-    out += [vm((3, 4, ROW, w), BF16) for w in WIDTH]
+    out += [vm((2, 4, ROW, w), BF16) for w in WIDTH]
+    out += [vm((2, 2, ROW, w), BF16) for w in WIDTH]
     out += [vm((3, ROW, w), BF16) for w in WIDTH]
     out += [vm((3, ROW, w), BF16) for w in WIDTH]
     out += [
-        vm((ROW, 640), F32),
-        vm((3, HALF, 640), F32),
+        vm((2, PAD, 640), BF16),
+        vm((3, PAD, 640), BF16),
         vm((DW, CAP), BF16),
         vm((DW, CAP), BF16),
         vm((CAP, DW), BF16),
-        dma((4,)),
+        dma((7,)),
     ]
-    for shape in ((9,), (3, 3), (3, 3), (3, 3), (3, 3), (3, 4, 2), (3, 4, 2), (3, 2), (3, 2), (3, 2, 4), (3, 3), (3, 3), (3, 3)):
+    for shape in (
+        (9,), (3, 3), (3, 3), (3, 3), (3, 4), (3, 4, 2), (3, 4, 2),
+        (3, 2), (3, 2), (3, 2, 4), (3, 4), (3, 3), (3, 3), (4,),
+    ):
         out += [dma(shape), dma(shape)]
     return out
 
 
-def finish(gw, gg, ga, loss, gw_out, gg_out, ga_out, loss_out, gw_v, ga_v, s_in, s_out):
+def finish(gw, gg, ga, loss, gw_out, gg_out, ga_out, loss_out, gw_v, gg_v, ga_v, loss_v, s_in, s_out):
     n = CAP // PARTS
-    pairs = [(gw, gw_v, gw_out)]
+    trips = []
     for k in range(PARTS):
         rows = slice(k * n, (k + 1) * n)
-        pairs.append((ga.at[rows], ga_v.at[rows], ga_out.at[rows]))
-    loads = [pltpu.make_async_copy(src, mid, s_in.at[i]) for i, (src, mid, _) in enumerate(pairs)]
-    stores = [pltpu.make_async_copy(mid, dst, s_out.at[i]) for i, (_, mid, dst) in enumerate(pairs)]
+        trips.append((ga.at[rows], ga_v.at[rows], ga_out.at[rows]))
+    trips += [(gw, gw_v, gw_out), (gg, gg_v, gg_out), (loss, loss_v, loss_out)]
+    loads = [pltpu.make_async_copy(src, mid, s_in.at[i]) for i, (src, mid, _) in enumerate(trips)]
+    stores = [pltpu.make_async_copy(mid, dst, s_out.at[i]) for i, (_, mid, dst) in enumerate(trips)]
     for copy in loads:
         copy.start()
-    gg_out[...] = gg[0, :]
-    loss_out[0, 0] = loss[0, 0]
     for load, store in zip(loads, stores):
         load.wait()
         store.start()
@@ -769,16 +832,15 @@
 def shards(attention_out, residual, target_rows, ref_logit, loss_weight, segment, counts, out_weight, norm_gain):
     any_ = pl.BlockSpec(memory_space=pl.ANY)
     vmem = pl.BlockSpec(memory_space=pltpu.VMEM)
-    smem = pl.BlockSpec(memory_space=pltpu.SMEM)
     gw, gg, ga, loss = pl.pallas_call(
         kernel,
         out_shape=(
             jax.ShapeDtypeStruct((HALF, DW), F32),
-            jax.ShapeDtypeStruct((1, DW), F32),
+            jax.ShapeDtypeStruct((DW,), F32),
             jax.ShapeDtypeStruct((CAP, DW), BF16),
-            jax.ShapeDtypeStruct((1, 128), F32),
+            jax.ShapeDtypeStruct((1, 1), F32),
         ),
-        in_specs=[any_, any_, any_, vmem, vmem, vmem, smem, vmem, vmem],
+        in_specs=[any_, any_, any_, vmem, vmem, vmem, vmem, vmem, vmem],
         out_specs=(vmem, vmem, any_, vmem),
         scratch_shapes=scratch(),
         compiler_params=pltpu.CompilerParams(
@@ -806,13 +868,15 @@
             jax.ShapeDtypeStruct((CAP, DW), BF16),
             jax.ShapeDtypeStruct((1, 1), F32),
         ),
-        in_specs=[any_, vmem, any_, vmem],
-        out_specs=(any_, vmem, any_, smem),
+        in_specs=[any_] * 4,
+        out_specs=(any_,) * 4,
         scratch_shapes=[
             pltpu.VMEM((HALF, DW), F32),
+            pltpu.VMEM((DW,), F32),
             pltpu.VMEM((CAP, DW), BF16),
-            pltpu.SemaphoreType.DMA((PARTS + 1,)),
-            pltpu.SemaphoreType.DMA((PARTS + 1,)),
+            pltpu.VMEM((1, 1), F32),
+            pltpu.SemaphoreType.DMA((PARTS + 3,)),
+            pltpu.SemaphoreType.DMA((PARTS + 3,)),
         ],
         compiler_params=pltpu.CompilerParams(vmem_limit_bytes=62 * 2**20),
     )(gw, gg, ga, loss)

time: 111 us -> 94.9 us (0.85)
  Pallas kernels: 109 us -> 93.2 us
    pallas_call x1, Pallas kernels: 105 us -> 89.9 us  [shards(): pl.pallas_call(kernel, out_shape=(jax.ShapeDtypeStruct((HALF, DW), F32),...]
where the time goes in v3:
time: 94.9 us; the launch traced here: 94.7 us
  Pallas kernels  93.2 us (98%)
  between operations  1.47 us (2%)
    pallas_call x1, Pallas kernels, shards(): pl.pallas_call(kernel, out_shape=(jax.ShapeDtypeStruct((HALF, DW), F32),...  89.9 us
    pallas_call x1, Pallas kernels, shards(): pl.pallas_call(finish, out_shape=(jax.ShapeDtypeStruct((HALF, DW), F32),...  3.35 us

profile of v3, /device:TPU:1, one launch (start us, length us, event | category | flops | bytes accessed | tf_op | source)
XLA Modules:
  0.0 94.7 jit_solution(6108204136568458224)
XLA Ops:
  1.3 89.9 %shard_map.120 = (f32[40,2560]{1,0:T(8,128)}, f32[2560]{0:T(1024)}, bf16[512,2560]{1,0:T(8,128)(2,1)}, f32[1,1]{1,0:T(1,128)}) custom-call(bf16[512,2560]{1,0:T(8,128)(2,1)} %a_hbm.1, bf16[512,2560]{1,0:T(8,128)(2,1)} %r_hbm.1, bf16[512,2560]{1,0:T(8,128)(2,1)} %t_hbm.1, f32[1,512]{1,0:T(1,128)} %ref_ref.1, s32[1,512]{1,0:T(1,128)} %lw_ref.1, ...), custom_call_target="tpu_custom_call" | custom-call | flops 20132659200 | bytes 10485760 | tf_op jit(solution)/shard_map/pallas_call | solution.py:835
  91.2 3.4 %shard_map.121 = (f32[40,2560]{1,0:T(8,128)}, f32[2560]{0:T(1024)}, bf16[512,2560]{1,0:T(8,128)(2,1)}, f32[1,1]{1,0:T(1,128)}) custom-call(f32[40,2560]{1,0:T(8,128)} %get-tuple-element.12.gw, f32[2560]{0:T(1024)} %get-tuple-element.13.gg, bf16[512,2560]{1,0:T(8,128)(2,1)} %get-tuple-element.14.ga, f32[1,1]{1,0:T(1,128)} %get-tuple-element.15.loss), custom_call_target="tpu_custom_call" | custom-call | tf_op jit(solution)/shard_map/pallas_call | solution.py:863

commit v4 on v3

--- a/solution.py
+++ b/solution.py
@@ -25,7 +25,7 @@
 NG = HC // GW
 WIDTH = (256, 256, 128)
 ORDER = (0, 1, 3, 2)
-PARTS = 8
+PARTS = 4
 
 
 def place():
@@ -42,16 +42,23 @@
     a_hbm,
     r_hbm,
     t_hbm,
+    ref_hbm,
+    lw_hbm,
+    seg_hbm,
+    cnt_hbm,
+    w_hbm,
+    gain_hbm,
+    gw_out,
+    gg_out,
+    ga_out,
+    loss_out,
     ref_ref,
     lw_ref,
     seg_ref,
     cnt_ref,
     w_ref,
     gain_in,
-    gw_out,
-    gg_out,
-    ga_out,
-    loss_out,
+    small,
     gain_row,
     gcol,
     a2,
@@ -151,6 +158,21 @@
 
     mine = pl.ds(pl.multiple_of(c * HC, 128), HC)
     theirs = pl.ds(pl.multiple_of((1 - c) * HC, 128), HC)
+    inputs = [
+        pltpu.make_async_copy(src, dst, small.at[i])
+        for i, (src, dst) in enumerate(
+            (
+                (w_hbm, w_ref),
+                (cnt_hbm, cnt_ref),
+                (ref_hbm, ref_ref),
+                (lw_hbm, lw_ref),
+                (seg_hbm, seg_ref),
+                (gain_hbm, gain_in),
+            )
+        )
+    ]
+    for copy in inputs:
+        copy.start()
     loads = [
         pltpu.make_async_copy(a_hbm, a2.at[0], loc.at[0]),
         pltpu.make_async_copy(t_hbm.at[:, mine], t2.at[0], loc.at[1]),
@@ -168,6 +190,8 @@
     for q in partners:
         pl.semaphore_signal(barrier, inc=1, device_id=q, device_id_type=MESH)
 
+    for copy in inputs:
+        copy.wait()
     lane = lax.broadcasted_iota(jnp.int32, (1, CAP), 1)
     live = lane < cnt_ref[...].reshape(1, 1)
     weight = jnp.where(live, lw_ref[...], 0).astype(F32)
@@ -342,19 +366,15 @@
     for copy in loads:
         copy.wait()
 
-    for p in pieces:
+    den_copies = [den_copies]
+
+    def spread_own(p):
         for d in (1, 3, 2):
             ph1[p, d].wait_recv()
         if p == 0:
-            den_copies = den_phase(1, den_total(0, den_copies))
+            den_copies.append(den_phase(1, den_total(0, den_copies[0])))
         for d in (1, 3):
             start(ph2[p, d])
-        if p == 0:
-            start(ph3[p, 0, 0])
-            start(ph3[p, 0, 1])
-    for p in (1, 2):
-        start(ph3[p, 0, 0])
-        start(ph3[p, 0, 1])
 
     def spread(p, d):
         if d == 2:
@@ -371,24 +391,28 @@
             ph3[p, d, s].wait_recv()
             start(ph4[p, d, s])
 
-    spread(0, 1)
-    spread(0, 3)
+    def arrived(p, steps):
+        for d in steps:
+            for s in (0, 1):
+                ph4[p, d, s].wait_recv()
+
     transpose_rows(0)
-    relay(0, 0)
-    for d in (1, 3):
-        spread(1, d)
-        spread(2, d)
-    den_copies = den_phase(2, den_total(1, den_copies))
+    spread_own(0)
+    start(ph3[0, 0, 0])
+    start(ph3[0, 0, 1])
+    spread_own(1)
+    spread_own(2)
+    start(ph3[2, 0, 0])
+    start(ph3[2, 0, 1])
     sib_a.wait_recv()
     transpose_rows(1)
-    spread(0, 2)
-    relay(0, 1)
-    relay(1, 0)
-    relay(2, 0)
-    forward(0, last_place(0, 0))
-    spread(1, 2)
-    spread(2, 2)
+    spread(0, 3)
+    spread(0, 1)
+    spread(2, 3)
     sib_t.wait_recv()
+    transpose_targets(0)
+    transpose_targets(1)
+    spread(2, 1)
     sib_res.wait_recv()
     for slot in (0, 1):
         part = jnp.zeros((CAP, 128), F32)
@@ -396,40 +420,50 @@
             cols = slice(k * 128, (k + 1) * 128)
             part += t2[slot, :, cols].astype(F32) * r2[slot, :, cols].astype(F32)
         sp[0, slot] = jnp.broadcast_to(jnp.sum(part.T, axis=0, keepdims=True), (8, CAP))
+    spread(1, 1)
+    spread(0, 2)
+    relay(2, 1)
+    relay(2, 0)
+    relay(2, 3)
+    spread(2, 2)
+    spread(1, 3)
+    den_copies = den_phase(2, den_total(1, den_copies[1]))
     relay(0, 3)
+    forward(2, last_place(2, 0))
+    forward(0, last_place(0, 0))
+    relay(0, 1)
+    near(2, 3, 1)
+    spread(1, 2)
+    relay(2, 2)
     forward(1, last_place(1, 0))
+    relay(0, 2)
+    relay(0, 0)
+    arrived(2, (1, 3))
+    near(2, 2, 1)
+    near(2, 1, 1)
+    start(ph3[1, 0, 0])
+    start(ph3[1, 0, 1])
+    forward(0, last_place(0, 1))
     relay(1, 1)
-    relay(2, 1)
-    transpose_targets(0)
-    transpose_targets(1)
-    forward(2, last_place(2, 0))
     relay(1, 3)
-    relay(2, 3)
+    near(2, 3, 0)
+    arrived(2, (0, 2))
+    near(2, 2, 0)
+    near(2, 1, 0)
+    relay(1, 2)
+    forward(0, last_place(0, 3))
+    near(1, 3, 1)
+    relay(1, 0)
     near(1, 1, 1)
-    near(1, 3, 1)
-    relay(0, 2)
-    forward(0, last_place(0, 1))
-    relay(1, 2)
-    relay(2, 2)
-    forward(0, last_place(0, 3))
-    near(2, 1, 1)
-    near(2, 3, 1)
-    for p in (1, 2):
-        near(p, 1, 0)
-        near(p, 3, 0)
-    denominator = jnp.maximum(den_total(2, den_copies)[0:1, 0:1], 1.0)
-    def arrived(p, steps):
-        for d in steps:
-            for s in (0, 1):
-                ph4[p, d, s].wait_recv()
-
+    near(1, 3, 0)
+    near(1, 1, 0)
+    arrived(1, (1, 3))
+    near(1, 2, 1)
     arrived(0, ORDER)
     forward(0, last_place(0, 2))
-    for odd in (1, 0):
-        for p in (1, 2):
-            arrived(p, (1, 3) if odd else (0, 2))
-            near(p, 2, odd)
-
+    arrived(1, (0, 2))
+    near(1, 2, 0)
+    denominator = jnp.maximum(den_total(2, den_copies)[0:1, 0:1], 1.0)
     stat[...] = jnp.zeros((2, 8, 2 * CAP), F32)
 
     @pl.loop(0, NG)
@@ -524,11 +558,11 @@
             to = peer(p, 0, 0, 1 + 2 * s)
             q0[p, s] = remote(st_o[p].at[:, half], rl[p].at[s], q0_s.at[p, s], q0_r.at[p, s], to)
             free = pl.ds(2 * (1 - s), 2)
-            qa[p, s] = remote(
-                st_n[p].at[s, :, free], rv[p].at[s, :, free], qa_s.at[p, s], qa_r.at[p, s], to
-            )
             for d in range(4):
                 i = (p2 + d) % 4
+                qa[p, s, d] = remote(
+                    st_n[p].at[s, i, free], rv[p].at[s, i, free], qa_s.at[p, s, d], qa_r.at[p, s, d], to
+                )
                 q1[p, s, d] = remote(
                     st_n[p].at[s, i, half], rv[p].at[s, i, half], q1_s.at[p, s, d], q1_r.at[p, s, d], to
                 )
@@ -570,38 +604,33 @@
             copy.wait_recv()
         return (gsum[axis, 0] + gsum[axis, 1]) + (gsum[axis, 2] + gsum[axis, 3])
 
-    gain_copies = gain_phase(0)
-
-    for p in (1, 2, 0):
+    waited = set()
+
+    def await_once(name, copy):
+        if name not in waited:
+            waited.add(name)
+            copy.wait_recv()
+
+    def first_blocks(p):
         grad_blocks(p, (pos(p)[2] + 2) % 4, put(st_o[p]))
         start(q0[p, 0])
         start(q0[p, 1])
 
-    for p in (1, 2, 0):
+    def near_blocks(p, t_):
+        grad_blocks(p, (pos(p)[2] + 1 + 2 * t_) % 4, put(st_n[p], (t_,)))
+        start(qa[p, t_, 2])
+        start(qa[p, t_, 1])
+
+    def relay_sum(p, d):
+        i = (pos(p)[1] + d) % 4
         for t_ in (0, 1):
-            grad_blocks(p, (pos(p)[2] + 1 + 2 * t_) % 4, put(st_n[p], (t_,)))
-            start(qa[p, t_])
-
-    def relay_sums(p):
-        for d in (2, 1, 3, 0):
-            i = (pos(p)[1] + d) % 4
-            for t_ in (0, 1):
-                if d == 2:
-                    q0[p, t_].wait_recv()
-                half = slice(2 * t_, 2 * t_ + 2)
-                both = st_n[p][t_, i, half].astype(F32) + rl[p][t_, i].astype(F32)
-                st_n[p][t_, i, half] = both.astype(BF16)
-                start(q1[p, t_, d])
-
-    for p in (1, 2):
-        grad_blocks(p, pos(p)[2], put(own[p]))
-    relay_sums(1)
-    relay_sums(2)
-    grad_blocks(0, pos(0)[2], put(own[0]))
-    relay_sums(0)
-
-    gsum[1, y] = gain_total(0, gain_copies)
-    gain_copies = gain_phase(1)
+            await_once(("q0", p, t_), q0[p, t_])
+            half = slice(2 * t_, 2 * t_ + 2)
+            both = st_n[p][t_, i, half].astype(F32) + rl[p][t_, i].astype(F32)
+            st_n[p][t_, i, half] = both.astype(BF16)
+            start(q1[p, t_, d])
+            if d in (1, 3):
+                start(qa[p, t_, 3 if d == 1 else 0])
 
     def lines(h, yy):
         m, n = yz[0]
@@ -619,14 +648,14 @@
             res = res + jnp.dot(w, right, preferred_element_type=F32)
         return res
 
-    ga_copies = []
+    ga_copies = {}
 
     def sibling_rows(yy):
         rows = slice(yy * 640, (yy + 1) * 640)
         ga_send[rows, :] = grad_rows(1, yy).astype(BF16)
         copy = remote(ga_send.at[rows], ga_recv.at[rows], ga_s.at[yy], ga_r.at[yy], sib)
         start(copy)
-        ga_copies.append(copy)
+        ga_copies[yy] = copy
 
     ga_stores = []
 
@@ -644,8 +673,7 @@
         p1, p2, p3 = pos(p)
         i = (p2 + d) % 4
         for t_ in (0, 1):
-            if d == 2:
-                qa[p, t_].wait_recv()
+            qa[p, t_, d].wait_recv()
             q1[p, t_, d].wait_recv()
         total = own[p][i] + rv[p][0, i].astype(F32) + rv[p][1, i].astype(F32)
         if d == 0:
@@ -698,40 +726,65 @@
         for copy in (last[p][1], last[p][2], last[p][0]):
             start(copy)
 
+    gain_copies = gain_phase(0)
+    first_blocks(1)
+    first_blocks(0)
+    first_blocks(2)
+    near_blocks(0, 1)
+    near_blocks(1, 0)
+    near_blocks(2, 0)
+    near_blocks(1, 1)
+    near_blocks(2, 1)
+    grad_blocks(2, pos(2)[2], put(own[2]))
+    relay_sum(1, 2)
+    relay_sum(2, 2)
+    near_blocks(0, 0)
+    relay_sum(2, 1)
+    relay_sum(0, 2)
+    relay_sum(1, 1)
     sibling_rows(0)
+    reduce_step(2, 2)
+    grad_blocks(1, pos(1)[2], put(own[1]))
+    relay_sum(1, 3)
+    reduce_step(1, 2)
+    relay_sum(0, 1)
+    relay_sum(2, 3)
+    grad_blocks(0, pos(0)[2], put(own[0]))
+    relay_sum(1, 0)
+    sibling_rows(3)
+    sibling_rows(2)
     sibling_rows(1)
-    sibling_rows(2)
-    sibling_rows(3)
-    reduce_step(1, 2)
-    reduce_step(2, 2)
-    own_rows(0)
-    own_rows(1)
+    relay_sum(0, 3)
+    relay_sum(2, 0)
     reduce_step(0, 2)
     reduce_step(1, 1)
+    gsum[1, y] = gain_total(0, gain_copies)
+    gain_copies = gain_phase(1)
+    reduce_step(1, 3)
+    own_rows(0)
+    reduce_step(1, 0)
     reduce_step(2, 1)
-    reduce_step(1, 3)
     reduce_step(2, 3)
+    relay_sum(0, 0)
+    reduce_step(0, 1)
+    reduce_step(0, 3)
+    second(1)
     gsum[2, z] = gain_total(1, gain_copies)
     gain_copies = gain_phase(2)
-    reduce_step(0, 1)
-    reduce_step(0, 3)
-    reduce_step(1, 0)
+    own_rows(2)
     reduce_step(2, 0)
+    second(2)
     reduce_step(0, 0)
-    second(1)
-    second(2)
     second(0)
     third(1)
     third(2)
-
     total = gain_total(2, gain_copies)
     gsib[c] = total
     gcopy = remote(gsib.at[c], gsib.at[c], sib_s.at[8], sib_r.at[8], sib)
     start(gcopy)
-
     third(0)
-    own_rows(2)
     own_rows(3)
+    own_rows(1)
 
     def place_columns(core, side, value):
         base = core * HC
@@ -763,6 +816,13 @@
     dma = pltpu.SemaphoreType.DMA
     vm = pltpu.VMEM
     out = [
+        vm((1, CAP), F32),
+        vm((1, CAP), jnp.int32),
+        vm((1, CAP), jnp.int32),
+        vm((1,), jnp.int32),
+        vm((HALF, DW), BF16),
+        vm((DW,), F32),
+        dma((6,)),
         vm((1, DW), F32),
         vm((NG, GW, 128), F32),
         vm((2, CAP, DW), BF16),
@@ -805,7 +865,7 @@
     ]
     for shape in (
         (9,), (3, 3), (3, 3), (3, 3), (3, 4), (3, 4, 2), (3, 4, 2),
-        (3, 2), (3, 2), (3, 2, 4), (3, 4), (3, 3), (3, 3), (4,),
+        (3, 2), (3, 2, 4), (3, 2, 4), (3, 4), (3, 3), (3, 3), (4,),
     ):
         out += [dma(shape), dma(shape)]
     return out
@@ -840,7 +900,7 @@
             jax.ShapeDtypeStruct((CAP, DW), BF16),
             jax.ShapeDtypeStruct((1, 1), F32),
         ),
-        in_specs=[any_, any_, any_, vmem, vmem, vmem, vmem, vmem, vmem],
+        in_specs=[any_] * 9,
         out_specs=(vmem, vmem, any_, vmem),
         scratch_shapes=scratch(),
         compiler_params=pltpu.CompilerParams(

time: 94.9 us -> 92.6 us (0.976)
  Pallas kernels: 93.2 us -> 90.9 us
    pallas_call x1, Pallas kernels: 89.9 us -> 87.5 us  [shards(): pl.pallas_call(kernel, out_shape=(jax.ShapeDtypeStruct((HALF, DW), F32),...]
where the time goes in v4:
time: 92.6 us; the launch traced here: 92.4 us
  Pallas kernels  90.9 us (98%)
  between operations  1.47 us (2%)
    pallas_call x1, Pallas kernels, shards(): pl.pallas_call(kernel, out_shape=(jax.ShapeDtypeStruct((HALF, DW), F32),...  87.5 us
    pallas_call x1, Pallas kernels, shards(): pl.pallas_call(finish, out_shape=(jax.ShapeDtypeStruct((HALF, DW), F32),...  3.4 us

profile of v4, /device:TPU:1, one launch (start us, length us, event | category | flops | bytes accessed | tf_op | source)
XLA Modules:
  0.0 92.4 jit_solution(3613469179852619251)
XLA Ops:
  1.3 87.5 %shard_map.120 = (f32[40,2560]{1,0:T(8,128)}, f32[2560]{0:T(1024)}, bf16[512,2560]{1,0:T(8,128)(2,1)}, f32[1,1]{1,0:T(1,128)}) custom-call(bf16[512,2560]{1,0:T(8,128)(2,1)} %a_hbm.1, bf16[512,2560]{1,0:T(8,128)(2,1)} %r_hbm.1, bf16[512,2560]{1,0:T(8,128)(2,1)} %t_hbm.1, f32[1,512]{1,0:T(1,128)} %ref_hbm.1, s32[1,512]{1,0:T(1,128)} %lw_hbm.1, ...), custom_call_target="tpu_custom_call" | custom-call | flops 20132659200 | bytes 10485760 | tf_op jit(solution)/shard_map/pallas_call | solution.py:895
  88.8 3.4 %shard_map.121 = (f32[40,2560]{1,0:T(8,128)}, f32[2560]{0:T(1024)}, bf16[512,2560]{1,0:T(8,128)(2,1)}, f32[1,1]{1,0:T(1,128)}) custom-call(f32[40,2560]{1,0:T(8,128)} %get-tuple-element.12.gw, f32[2560]{0:T(1024)} %get-tuple-element.13.gg, bf16[512,2560]{1,0:T(8,128)(2,1)} %get-tuple-element.14.ga, f32[1,1]{1,0:T(1,128)} %get-tuple-element.15.loss), custom_call_target="tpu_custom_call" | custom-call | tf_op jit(solution)/shard_map/pallas_call | solution.py:923

commit v5 on v4

--- a/solution.py
+++ b/solution.py
@@ -391,6 +391,19 @@
             ph3[p, d, s].wait_recv()
             start(ph4[p, d, s])
 
+    stat[...] = jnp.zeros((2, 8, 2 * CAP), F32)
+
+    def token_sums(low, high):
+        @pl.loop(low, high)
+        def _(g):
+            for slot in (0, 1):
+                cols = slice(slot * CAP, (slot + 1) * CAP)
+                gains = jnp.concatenate([gcol[g]] * 4, axis=1)
+                p_ = pr[g, :, cols]
+                stat[0, :, cols] += jnp.sum((p_ * p_).reshape(GW // 8, 8, CAP), axis=0)
+                tp = p_ * tt[g, :, cols].astype(F32) * gains
+                stat[1, :, cols] += jnp.sum(tp.reshape(GW // 8, 8, CAP), axis=0)
+
     def arrived(p, steps):
         for d in steps:
             for s in (0, 1):
@@ -450,6 +463,7 @@
     arrived(2, (0, 2))
     near(2, 2, 0)
     near(2, 1, 0)
+    token_sums(4, NG)
     relay(1, 2)
     forward(0, last_place(0, 3))
     near(1, 3, 1)
@@ -461,20 +475,11 @@
     near(1, 2, 1)
     arrived(0, ORDER)
     forward(0, last_place(0, 2))
+    token_sums(0, 2)
     arrived(1, (0, 2))
     near(1, 2, 0)
     denominator = jnp.maximum(den_total(2, den_copies)[0:1, 0:1], 1.0)
-    stat[...] = jnp.zeros((2, 8, 2 * CAP), F32)
-
-    @pl.loop(0, NG)
-    def _(g):
-        for slot in (0, 1):
-            cols = slice(slot * CAP, (slot + 1) * CAP)
-            gains = jnp.concatenate([gcol[g]] * 4, axis=1)
-            p_ = pr[g, :, cols]
-            stat[0, :, cols] += jnp.sum((p_ * p_).reshape(GW // 8, 8, CAP), axis=0)
-            tp = p_ * tt[g, :, cols].astype(F32) * gains
-            stat[1, :, cols] += jnp.sum(tp.reshape(GW // 8, 8, CAP), axis=0)
+    token_sums(2, 4)
 
     row = lax.broadcasted_iota(jnp.int32, (8, CAP), 0)
     for slot in (0, 1):
@@ -514,24 +519,20 @@
         alpha[slot] = jnp.broadcast_to(grad / scale, (8, CAP))
         beta[slot] = jnp.broadcast_to(q3 / (scale * scale * DW), (8, CAP))
 
-    @pl.loop(0, NG)
-    def _(g):
-        gains = jnp.concatenate([gcol[g]] * 4, axis=1)
-        part = jnp.zeros((GW, 128), F32)
-        for slot in (0, 1):
-            cols = slice(slot * CAP, (slot + 1) * CAP)
-            al, be = alpha[slot, 0:1], beta[slot, 0:1]
-            p_ = pr[g, :, cols]
-            t = tt[g, :, cols].astype(F32)
-            pg[g, :, cols] = (al * (t * gains - p_ * be)).astype(BF16)
-            u = al * t * p_
-            part += (u[:, 0:128] + u[:, 128:256]) + (u[:, 256:384] + u[:, 384:512])
-        gacc[g] = part
-
-    @pl.loop(0, NG)
-    def _(g):
-        cols = pl.ds(pl.multiple_of(g * GW, GW), GW)
-        gsum[0, x, 0:1, cols] = jnp.sum(gacc[g].T, axis=0, keepdims=True)
+    def gradient(low, high):
+        @pl.loop(low, high)
+        def _(g):
+            gains = jnp.concatenate([gcol[g]] * 4, axis=1)
+            part = jnp.zeros((GW, 128), F32)
+            for slot in (0, 1):
+                cols = slice(slot * CAP, (slot + 1) * CAP)
+                al, be = alpha[slot, 0:1], beta[slot, 0:1]
+                p_ = pr[g, :, cols]
+                t = tt[g, :, cols].astype(F32)
+                pg[g, :, cols] = (al * (t * gains - p_ * be)).astype(BF16)
+                u = al * t * p_
+                part += (u[:, 0:128] + u[:, 128:256]) + (u[:, 256:384] + u[:, 384:512])
+            gacc[g] = part
 
     def grad_blocks(p, v, emit):
         m, n = yz[p]
@@ -726,10 +727,19 @@
         for copy in (last[p][1], last[p][2], last[p][0]):
             start(copy)
 
+    gradient(2, 4)
+    first_blocks(1)
+    gradient(0, 2)
+    first_blocks(0)
+    gradient(4, NG)
+    first_blocks(2)
+
+    @pl.loop(0, NG)
+    def _(g):
+        cols = pl.ds(pl.multiple_of(g * GW, GW), GW)
+        gsum[0, x, 0:1, cols] = jnp.sum(gacc[g].T, axis=0, keepdims=True)
+
     gain_copies = gain_phase(0)
-    first_blocks(1)
-    first_blocks(0)
-    first_blocks(2)
     near_blocks(0, 1)
     near_blocks(1, 0)
     near_blocks(2, 0)

time: 92.6 us -> 90.9 us (0.982)
  Pallas kernels: 90.9 us -> 89.2 us
    pallas_call x1, Pallas kernels: 87.5 us -> 85.8 us  [shards(): pl.pallas_call(kernel, out_shape=(jax.ShapeDtypeStruct((HALF, DW), F32),...]
where the time goes in v5:
time: 90.9 us; the launch traced here: 90.7 us
  Pallas kernels  89.2 us (98%)
  between operations  1.45 us (2%)
    pallas_call x1, Pallas kernels, shards(): pl.pallas_call(kernel, out_shape=(jax.ShapeDtypeStruct((HALF, DW), F32),...  85.8 us
    pallas_call x1, Pallas kernels, shards(): pl.pallas_call(finish, out_shape=(jax.ShapeDtypeStruct((HALF, DW), F32),...  3.4 us

profile of v5, /device:TPU:1, one launch (start us, length us, event | category | flops | bytes accessed | tf_op | source)
XLA Modules:
  0.0 90.7 jit_solution(4248748861120398219)
XLA Ops:
  1.3 85.8 %shard_map.120 = (f32[40,2560]{1,0:T(8,128)}, f32[2560]{0:T(1024)}, bf16[512,2560]{1,0:T(8,128)(2,1)}, f32[1,1]{1,0:T(1,128)}) custom-call(bf16[512,2560]{1,0:T(8,128)(2,1)} %a_hbm.1, bf16[512,2560]{1,0:T(8,128)(2,1)} %r_hbm.1, bf16[512,2560]{1,0:T(8,128)(2,1)} %t_hbm.1, f32[1,512]{1,0:T(1,128)} %ref_hbm.1, s32[1,512]{1,0:T(1,128)} %lw_hbm.1, ...), custom_call_target="tpu_custom_call" | custom-call | flops 20132659200 | bytes 10485760 | tf_op jit(solution)/shard_map/pallas_call | solution.py:905
  87.1 3.4 %shard_map.121 = (f32[40,2560]{1,0:T(8,128)}, f32[2560]{0:T(1024)}, bf16[512,2560]{1,0:T(8,128)(2,1)}, f32[1,1]{1,0:T(1,128)}) custom-call(f32[40,2560]{1,0:T(8,128)} %get-tuple-element.12.gw, f32[2560]{0:T(1024)} %get-tuple-element.13.gg, bf16[512,2560]{1,0:T(8,128)(2,1)} %get-tuple-element.14.ga, f32[1,1]{1,0:T(1,128)} %get-tuple-element.15.loss), custom_call_target="tpu_custom_call" | custom-call | tf_op jit(solution)/shard_map/pallas_call | solution.py:933
